TPU v7x, 512 devices: a whole 4x8x8 slice. The times are simulated.
512 devices in a mesh: depth: 8 (over z), lat: 64 (over y, x, core).
Axes of the slice: x: 4, y: 8, z: 8, core: 2. Of those that a mesh axis runs over, the one named last changes fastest.
Arguments:
- volume: bfloat16 [8, 4096, 4096], P('depth', 'lat'), may hold values from -6 to 6
- hologram: bfloat16 [4096, 4096], P('lat'), may hold values from -6 to 6
- plane_depth: float32 [8], P('depth'), may hold values from 1 to 4
- tile_list: int32 [8, 32, 16], P('depth'), may hold values from 0 to 32, as said below
Outputs:
- new_volume: float32 [8, 4096, 4096], P('depth', 'lat')
Inputs may be any that keep to these rules, and one draw needn't show every extreme that they name: `tile_list`: each list names distinct column tiles; the value 32 marks an unused slot, and unused slots come after the used ones; every plane has a tile row whose list is full and one that names a single tile.
All inputs are finite; a program needn't handle non-finite values.
Results may differ from a plain program's by a relative error of at most 0.0003.
Values sent between devices are 32-bit elements; how exact they have to be, the bound alone decides.
No kernel may reach another device: no remote copies, remote signals or barrier semaphores. Data moves between devices by JAX's collectives and lax.ppermute only.
A program may use at most 64 MiB of HBM per device.

v0:
```python
import math

import jax
import jax.numpy as jnp
from jax import lax
from jax.sharding import PartitionSpec as P

TILE = 128


TWO_PI = 2.0 * math.pi
WAVE_RATIO = 0.266
DEPTH_SCALE = 0.001 / 5.32e-07
STEP_SIZE = 0.1
THRESHOLD = 0.25


def signed_freq(index_ids, length):
    return jnp.where(index_ids < length // 2, index_ids, index_ids - length)


def bending_table(row_freq, col_freq, total_rows, total_cols):
    freq_rows = signed_freq(row_freq, total_rows).astype(jnp.float32) * (WAVE_RATIO / total_rows)
    freq_cols = signed_freq(col_freq, total_cols).astype(jnp.float32) * (WAVE_RATIO / total_cols)
    squared = freq_rows[:, None] * freq_rows[:, None] + freq_cols[None, :] * freq_cols[None, :]
    return squared / (1.0 + jnp.sqrt(1.0 - squared))


def phasor(first_len, second_len, period, direction):
    left_ids = lax.broadcasted_iota(jnp.int32, (first_len, second_len), 0)
    right_ids = lax.broadcasted_iota(jnp.int32, (first_len, second_len), 1)
    angles = (left_ids * right_ids % period).astype(jnp.float32) * (direction * TWO_PI / period)
    return (jnp.cos(angles), jnp.sin(angles))


def product(pattern, left_arr, right_arr):
    return jnp.einsum(
        pattern,
        left_arr,
        right_arr,
        precision=lax.Precision.HIGHEST,
        preferred_element_type=jnp.float32,
    )


def joined_mix(with_cos, with_sin):
    half = with_cos.shape[-1] // 2
    real_part = with_cos[..., :half] - with_sin[..., half:]
    imag_part = with_cos[..., half:] + with_sin[..., :half]
    return jnp.concatenate([real_part, imag_part], axis=-1)


def contract(pattern, joined, phasors):
    cos_table, sin_table = phasors
    return joined_mix(product(pattern, joined, cos_table), product(pattern, joined, sin_table))


def rotate(joined, cos_table, sin_table):
    half = joined.shape[-1] // 2
    real_part = joined[..., :half]
    imag_part = joined[..., half:]
    return jnp.concatenate(
        [
            real_part * cos_table - imag_part * sin_table,
            real_part * sin_table + imag_part * cos_table,
        ],
        axis=-1,
    )


def block_table(width, direction):
    cos_table, sin_table = phasor(width, width, width, direction)
    upper = jnp.concatenate([cos_table, sin_table], axis=1)
    lower = jnp.concatenate([-sin_table, cos_table], axis=1)
    return jnp.concatenate([upper, lower], axis=0)


def columns_forward(spatial, lane_count):
    plane_count, row_count, total_len = spatial.shape
    col_width = total_len // lane_count
    blocked = spatial.reshape(plane_count, row_count, lane_count, col_width)
    cos_table, sin_table = phasor(lane_count, lane_count, lane_count, -1.0)
    stacked = jnp.stack([cos_table, sin_table], axis=2)
    joined = product("prab,akc->pkrcb", blocked, stacked).reshape(
        plane_count, lane_count, row_count, 2 * col_width
    )
    twist_cos, twist_sin = phasor(lane_count, col_width, total_len, -1.0)
    joined = rotate(joined, twist_cos[:, None, :], twist_sin[:, None, :])
    return product("pkrx,xy->pkry", joined, block_table(col_width, -1.0))


def rows_forward(joined, lane_count):
    plane_count, lanes_in, row_count, doubled = joined.shape
    total_len = lane_count * row_count
    joined = contract("pjrx,jk->pkrx", joined, phasor(lane_count, lane_count, lane_count, -1.0))
    twist_cos, twist_sin = phasor(lane_count, row_count, total_len, -1.0)
    joined = rotate(joined, twist_cos[:, :, None], twist_sin[:, :, None])
    joined = contract("pkrx,rm->pmkx", joined, phasor(row_count, row_count, row_count, -1.0))
    return joined.reshape(plane_count, total_len, doubled)


def rows_inverse(joined, lane_count):
    plane_count, total_len, doubled = joined.shape
    row_count = total_len // lane_count
    joined = joined.reshape(plane_count, row_count, lane_count, doubled)
    joined = contract("pmkx,mb->pbkx", joined, phasor(row_count, row_count, row_count, 1.0))
    twist_cos, twist_sin = phasor(row_count, lane_count, total_len, 1.0)
    joined = rotate(joined, twist_cos[:, :, None], twist_sin[:, :, None])
    joined = contract("pbkx,ka->pabx", joined, phasor(lane_count, lane_count, lane_count, 1.0))
    return joined * (1.0 / total_len)


def columns_inverse_real(joined):
    plane_count, lane_count, row_count, doubled = joined.shape
    col_width = doubled // 2
    total_len = lane_count * col_width
    joined = product("pkrx,xy->pkry", joined, block_table(col_width, 1.0))
    twist_cos, twist_sin = phasor(lane_count, col_width, total_len, 1.0)
    joined = rotate(joined, twist_cos[:, None, :], twist_sin[:, None, :])
    last_cos, last_sin = phasor(lane_count, lane_count, lane_count, 1.0)
    stacked = jnp.stack([last_cos, -last_sin], axis=2)
    spatial = product(
        "pkrcb,kac->prab", joined.reshape(plane_count, lane_count, row_count, 2, col_width), stacked
    )
    return spatial.reshape(plane_count, row_count, total_len) * (1.0 / total_len)


def body(volume, hologram, plane_depth, tile_list):
    lane_count = lax.axis_size("lat")
    lat_place = lax.axis_index("lat")
    plane_count, row_count, total_cols = volume.shape
    col_width = total_cols // lane_count
    total_rows = row_count * lane_count
    row_ids = lat_place * row_count + lax.iota(jnp.int32, row_count)
    listed = jnp.take(tile_list, row_ids // TILE, axis=1)
    tile_ids = lax.iota(jnp.int32, total_cols // TILE)
    tile_hits = jnp.any(listed[:, :, :, None] == tile_ids[None, None, None, :], axis=2)
    support = jnp.broadcast_to(
        tile_hits[:, :, :, None], (plane_count, row_count, total_cols // TILE, TILE)
    )
    support = support.reshape(plane_count, row_count, total_cols).astype(jnp.float32)
    current = volume.astype(jnp.float32) * support
    row_freq = lax.iota(jnp.int32, total_rows)
    col_freq = lat_place + lane_count * lax.iota(jnp.int32, col_width)
    bending = bending_table(row_freq, col_freq, total_rows, total_cols)
    phases = -(TWO_PI * DEPTH_SCALE * plane_depth)[:, None, None] * bending[None, :, :]
    wave_cos = jnp.cos(phases)
    wave_sin = jnp.sin(phases)
    spectrum = columns_forward(current, lane_count)
    spectrum = lax.all_to_all(spectrum, "lat", split_axis=1, concat_axis=1, tiled=True)
    spectrum = rows_forward(spectrum, lane_count)
    spectrum = rotate(spectrum, wave_cos, wave_sin)
    back = rows_inverse(spectrum, lane_count)
    back = lax.all_to_all(back, "lat", split_axis=1, concat_axis=1, tiled=True)
    share_rows = row_count // lax.axis_size("depth")
    field_sum = lax.psum_scatter(
        2.0 * jnp.sum(columns_inverse_real(back), axis=0), "depth", scatter_dimension=0, tiled=True
    )
    observed = lax.dynamic_slice_in_dim(
        hologram, lax.axis_index("depth") * share_rows, share_rows, 0
    )
    residual = observed.astype(jnp.float32) - field_sum
    res_spec = columns_forward(residual[None], lane_count)
    res_spec = lax.all_to_all(res_spec, "lat", split_axis=1, concat_axis=1, tiled=True)
    res_spec = lax.all_gather(res_spec, "depth", axis=2, tiled=True)
    res_spec = rows_forward(res_spec, lane_count)
    adjoint = rotate(res_spec, wave_cos, -wave_sin)
    grad_scale = 2.0
    adjoint = rows_inverse(adjoint, lane_count)
    adjoint = lax.all_to_all(adjoint, "lat", split_axis=1, concat_axis=1, tiled=True)
    gradient = grad_scale * columns_inverse_real(adjoint)
    updated = current + STEP_SIZE * gradient
    return support * (updated - jnp.clip(updated, -THRESHOLD, THRESHOLD))


def solution(mesh):
    return jax.shard_map(
        body,
        mesh=mesh,
        in_specs=(P("depth", "lat", None), P("lat", None), P("depth"), P("depth", None, None)),
        out_specs=P("depth", "lat", None),
        check_vma=False,
    )
```

profile of v0, /device:TPU:1, one launch (start us, length us, event | category | flops | bytes accessed | tf_op | source)
XLA Modules:
  0.0 464.4 jit_solution(15727203543235053918)
XLA Ops:
  10.7 1.2 convert_select_fusion
  12.8 4.3 convolution_bitcast_fusion
  17.1 5.2 %copy.227 = f32[1,64,64,2,64]{4,3,2,1,0:T(2,128)} copy(f32[1,64,64,2,64]{4,1,2,3,0:T(8,128)S(1)} %convolution_bitcast_fusion) | data formatting | bytes 4194304 | tf_op jit(solution)/shard_map/prab,akc->pkrcb/transpose | solution.py:37
  22.3 4.7 %reshape.657 = f32[1,64,64,128]{3,2,1,0:T(8,128)S(1)} reshape(f32[1,64,64,2,64]{4,3,2,1,0:T(2,128)} %copy.227) | data formatting | bytes 4194304 | tf_op jit(solution)/shard_map/reshape | solution.py:84
  27.1 0.8 multiply_subtract_fusion.6
  27.9 3.3 fusion.101
  31.2 11.6 %all-to-all-start = ((f32[1,64,64,128]{3,2,0,1:T(8,128)}), f32[1,64,64,128]{3,2,0,1:T(8,128)S(1)}, u32[]{:S(2)}, u32[]{:S(2)}) async-start(f32[1,64,64,128]{3,2,0,1:T(8,128)} %fusion.101), calls=%async_computation | async-start | bytes 4194304 | tf_op jit(solution)/shard_map/all_to_all | solution.py:150
  45.8 46.7 %all-to-all-done = f32[1,64,64,128]{3,2,0,1:T(8,128)S(1)} async-done(((f32[1,64,64,128]{3,2,0,1:T(8,128)}), f32[1,64,64,128]{3,2,0,1:T(8,128)S(1)}, u32[]{:S(2)}, u32[]{:S(2)}) %all-to-all-start) | async-done | bytes 2097184 | tf_op jit(solution)/shard_map/all_to_all | solution.py:150
  92.5 3.2 fusion.83
  95.7 3.1 fusion.86
  98.9 2.7 multiply_subtract_fusion.5
  102.1 3.2 fusion.47
  105.3 3.1 fusion.50
  108.5 1.1 slice_subtract_fusion.6
  110.2 1.2 copy.238
  111.5 2.0 fusion.227
  113.5 2.2 copy.312
  115.6 1.6 copy.313
  117.2 5.8 %multiply_subtract_fusion.8 = (f32[1,4096,64]{1,2,0:T(8,128)S(1)}, f32[1,4096,64]{1,2,0:T(8,128)S(1)}) fusion(f32[1,4096,64]{1,2,0:T(8,128)} %copy.313, f32[1,4096,64]{1,2,0:T(8,128)S(1)} %copy.312, f32[64]{0:T(128)} %fusion.153, f32[4096]{0:T(1024)S(1)} %fusion.147, f32[]{:T(128)} %bitcast.29), kind=kLoop, calls=%fused_computation.125 | loop fusion | flops 2883584 | bytes 4210948 | tf_op jit(solution)/shard_map/sub | solution.py:64
  123.0 1.5 pad_maximum_fusion.1
  124.5 1.9 copy.241
  126.5 3.2 fusion.53
  129.6 3.2 fusion.56
  132.8 2.9 multiply_subtract_fusion.4
  136.3 3.1 fusion.59
  139.5 3.2 fusion.62
  142.7 1.1 slice_subtract_fusion.4
  144.4 2.6 copy.252
  147.0 7.0 %all-to-all-start.1 = ((f32[1,64,64,128]{3,2,0,1:T(8,128)}), f32[1,64,64,128]{3,2,0,1:T(8,128)S(1)}, u32[]{:S(2)}, u32[]{:S(2)}) async-start(f32[1,64,64,128]{3,2,0,1:T(8,128)} %copy.252), calls=%async_computation.1 | async-start | bytes 4194304 | tf_op jit(solution)/shard_map/all_to_all | solution.py:154
  154.7 49.0 %all-to-all-done.1 = f32[1,64,64,128]{3,2,0,1:T(8,128)S(1)} async-done(((f32[1,64,64,128]{3,2,0,1:T(8,128)}), f32[1,64,64,128]{3,2,0,1:T(8,128)S(1)}, u32[]{:S(2)}, u32[]{:S(2)}) %all-to-all-start.1) | async-done | bytes 2097184 | tf_op jit(solution)/shard_map/all_to_all | solution.py:154
  203.7 1.9 fusion.89
  205.6 0.8 multiply_subtract_fusion.3
  207.0 3.7 reshape.665
  210.8 7.2 %fusion.14 = f32[1,64,64,64]{3,2,1,0:T(8,128)S(1)} fusion(f32[64,64,2,64]{3,2,1,0:T(2,128)} %reshape.665, f32[64,64,1]{0,1,2:T(8,128)S(1)} %get-tuple-element.47, f32[64,64,1]{0,1,2:T(8,128)S(1)} %get-tuple-element.48), kind=kOutput, calls=%fused_computation.47 | convolution fusion | flops 402923520 | bytes 3178496 | tf_op jit(solution)/shard_map/pkrcb,kac->prab/dot_general | solution.py:37
  218.0 1.6 mul.875
  219.7 38.5 %reduce-scatter.2.cloned.1.call-done = f32[8,4096]{1,0:T(8,128)} async-done(((f32[64,4096]{1,0:T(8,128)}), f32[8,4096]{1,0:T(8,128)}) %reduce-scatter.2.cloned.1.call-update) | async-done | bytes 131088 | tf_op jit(solution)/shard_map/reduce_scatter | solution.py:156
  258.2 0.9 convert_subtract_fusion
  261.2 27.9 %all_to_all.20 = f32[1,64,8,128]{3,2,0,1:T(8,128)S(1)} all-to-all(f32[1,64,8,128]{3,2,0,1:T(8,128)S(1)} %convolution_bitcast_fusion.2), channel_id=1, replica_groups=mesh['depth'=8,'lat'=64] {'lat'}, dimensions={1} | all-to-all | bytes 524288 | tf_op jit(solution)/shard_map/all_to_all | solution.py:164
  289.9 33.3 %all-gather.2.cloned.1.call-done = f32[1,64,64,128]{3,1,0,2:T(8,128)} async-done(((f32[1,64,8,128]{3,1,0,2:T(8,128)}), f32[1,64,64,128]{3,1,0,2:T(8,128)}) %all-gather.2.cloned.1.call-update) | async-done | bytes 2097168 | tf_op jit(solution)/shard_map/all_gather | solution.py:165
  323.2 3.8 fusion.92
  327.0 2.0 fusion.95
  329.1 2.7 multiply_subtract_fusion.2
  332.4 3.2 fusion.65
  335.5 3.1 fusion.68
  338.7 1.1 slice_subtract_fusion.2
  340.5 1.2 copy.263
  341.7 2.0 fusion.226
  343.7 2.2 copy.314
  345.9 1.6 copy.315
  347.5 6.0 %multiply_subtract_fusion.7 = (f32[1,4096,64]{1,2,0:T(8,128)S(1)}, f32[1,4096,64]{1,2,0:T(8,128)S(1)}) fusion(f32[1,4096,64]{1,2,0:T(8,128)} %copy.315, f32[1,4096,64]{1,2,0:T(8,128)S(1)} %copy.314, f32[64]{0:T(128)S(1)} %copy-done.27, f32[4096]{0:T(1024)S(1)} %fusion.147, f32[]{:T(128)} %bitcast.29), kind=kLoop, calls=%fused_computation.123 | loop fusion | flops 3145728 | bytes 4210948 | tf_op jit(solution)/shard_map/sub | solution.py:64
  353.5 1.5 pad_maximum_fusion.4
  355.0 1.9 copy.266
  356.9 3.2 fusion.71
  360.1 3.1 fusion.74
  363.3 2.7 multiply_subtract_fusion.1
  366.6 3.2 fusion.77
  369.7 3.1 fusion.80
  372.9 1.1 slice_subtract_fusion
  374.6 1.2 copy.275
  375.9 64.2 %all_to_all.21 = f32[1,64,64,128]{3,2,0,1:T(8,128)S(1)} all-to-all(f32[1,64,64,128]{3,2,0,1:T(8,128)S(1)} %copy.275), channel_id=1, replica_groups=mesh['depth'=8,'lat'=64] {'lat'}, dimensions={1} | all-to-all | bytes 4194304 | tf_op jit(solution)/shard_map/all_to_all | solution.py:170
  440.1 1.9 fusion.98
  443.5 3.7 reshape.675
  447.2 7.2 %fusion.7 = f32[1,64,64,64]{3,2,1,0:T(8,128)S(1)} fusion(f32[64,64,2,64]{3,2,1,0:T(2,128)} %reshape.675, f32[64,64,1]{0,1,2:T(8,128)S(1)} %copy-done.10, f32[64,64,1]{0,1,2:T(8,128)S(1)} %copy-done.12), kind=kOutput, calls=%fused_computation.39 | convolution fusion | flops 402923520 | bytes 3178496 | tf_op jit(solution)/shard_map/pkrcb,kac->prab/dot_general | solution.py:37
  455.1 2.3 fusion.109
  (105 shorter events, 18.4 us)
Async XLA Ops:
  7.6 20.3 %copy-start.19 = (f32[64,64]{1,0:T(8,128)}, f32[64,64]{1,0:T(8,128)S(1)}, u32[]{:S(2)}) copy-start(f32[64,64]{1,0:T(8,128)S(1)} %get-tuple-element.41) | copy-start | bytes 49156
  7.7 20.3 %copy-start.21 = (f32[64,64]{1,0:T(8,128)}, f32[64,64]{1,0:T(8,128)S(1)}, u32[]{:S(2)}) copy-start(f32[64,64]{1,0:T(8,128)S(1)} %get-tuple-element.42) | copy-start | bytes 49156
  27.0 0.9 copy-start.23
  31.2 61.3 %all-to-all-start = ((f32[1,64,64,128]{3,2,0,1:T(8,128)}), f32[1,64,64,128]{3,2,0,1:T(8,128)S(1)}, u32[]{:S(2)}, u32[]{:S(2)}) async-start(f32[1,64,64,128]{3,2,0,1:T(8,128)} %fusion.101), calls=%async_computation | async-start | bytes 4194304 | tf_op jit(solution)/shard_map/all_to_all | solution.py:150
  42.9 55.9 %copy-start.5 = (f32[64,64]{0,1:T(8,128)}, f32[64,64]{0,1:T(8,128)S(1)}, u32[]{:S(2)}) copy-start(f32[64,64]{0,1:T(8,128)S(1)} %copy.232) | copy-start | bytes 49156
  43.0 55.9 %copy-start.7 = (f32[64,64]{0,1:T(8,128)}, f32[64,64]{0,1:T(8,128)S(1)}, u32[]{:S(2)}) copy-start(f32[64,64]{0,1:T(8,128)S(1)} %copy.233) | copy-start | bytes 49156
  129.6 3.2 copy-start.1
  129.6 3.2 copy-start.3
  147.0 56.7 %all-to-all-start.1 = ((f32[1,64,64,128]{3,2,0,1:T(8,128)}), f32[1,64,64,128]{3,2,0,1:T(8,128)S(1)}, u32[]{:S(2)}, u32[]{:S(2)}) async-start(f32[1,64,64,128]{3,2,0,1:T(8,128)} %copy.252), calls=%async_computation.1 | async-start | bytes 4194304 | tf_op jit(solution)/shard_map/all_to_all | solution.py:154
  154.0 104.2 %reduce-scatter.2.cloned.1.call-start = ((), (), s32[]{:S(2)}) async-start(), calls=%async_computation.5 | async-start | bytes 1179648 | tf_op jit(solution)/shard_map/reduce_scatter | solution.py:156
  154.4 51.2 %copy-start.13 = (f32[64,64]{1,0:T(8,128)}, f32[64,64]{1,0:T(8,128)S(1)}, u32[]{:S(2)}) copy-start(f32[64,64]{1,0:T(8,128)S(1)} %fusion.148) | copy-start | bytes 49156
  154.5 51.0 %copy-start.15 = (f32[64,64]{1,0:T(8,128)}, f32[64,64]{1,0:T(8,128)S(1)}, u32[]{:S(2)}) copy-start(f32[64,64]{1,0:T(8,128)S(1)} %get-tuple-element.43) | copy-start | bytes 49156
  154.6 51.0 %copy-start.17 = (f32[64,64]{1,0:T(8,128)}, f32[64,64]{1,0:T(8,128)S(1)}, u32[]{:S(2)}) copy-start(f32[64,64]{1,0:T(8,128)S(1)} %get-tuple-element.44) | copy-start | bytes 49156
  154.7 56.1 %copy-start.9 = (f32[64,64,1]{0,1,2:T(8,128)}, f32[64,64,1]{0,1,2:T(8,128)S(1)}, u32[]{:S(2)}) copy-start(f32[64,64,1]{0,1,2:T(8,128)S(1)} %get-tuple-element.47) | copy-start | bytes 49156
  154.7 56.0 %copy-start.11 = (f32[64,64,1]{0,1,2:T(8,128)}, f32[64,64,1]{0,1,2:T(8,128)S(1)}, u32[]{:S(2)}) copy-start(f32[64,64,1]{0,1,2:T(8,128)S(1)} %get-tuple-element.48) | copy-start | bytes 49156
  218.0 41.3 %copy-start.25 = (f32[64,64,1]{0,1,2:T(8,128)S(1)}, f32[64,64,1]{0,1,2:T(8,128)}, u32[]{:S(2)}) copy-start(f32[64,64,1]{0,1,2:T(8,128)} %get-tuple-element.37) | copy-start | bytes 49156
  218.0 41.3 %copy-start.26 = (f32[64,64,1]{0,1,2:T(8,128)S(1)}, f32[64,64,1]{0,1,2:T(8,128)}, u32[]{:S(2)}) copy-start(f32[64,64,1]{0,1,2:T(8,128)} %get-tuple-element.38) | copy-start | bytes 49156
  219.6 103.6 %all-gather.2.cloned.1.call-start = ((), (), s32[]{:S(2)}) async-start(), calls=%async_computation.6 | async-start | bytes 2359296 | tf_op jit(solution)/shard_map/all_gather | solution.py:165
  259.1 1.6 copy-start.20
  259.1 1.6 copy-start.22
  259.1 1.6 copy-start.24
  323.2 3.8 copy-start
  327.0 2.1 copy-start.6
  327.0 2.1 copy-start.8
  345.9 1.6 copy-start.27
  360.1 3.2 copy-start.2
  360.1 3.2 copy-start.4
  375.9 64.3 %copy-start.14 = (f32[64,64]{1,0:T(8,128)S(1)}, f32[64,64]{1,0:T(8,128)}, u32[]{:S(2)}) copy-start(f32[64,64]{1,0:T(8,128)} %copy-done.13) | copy-start | bytes 49156
  375.9 64.3 %copy-start.16 = (f32[64,64]{1,0:T(8,128)S(1)}, f32[64,64]{1,0:T(8,128)}, u32[]{:S(2)}) copy-start(f32[64,64]{1,0:T(8,128)} %copy-done.15) | copy-start | bytes 49156
  375.9 64.3 %copy-start.18 = (f32[64,64]{1,0:T(8,128)S(1)}, f32[64,64]{1,0:T(8,128)}, u32[]{:S(2)}) copy-start(f32[64,64]{1,0:T(8,128)} %copy-done.17) | copy-start | bytes 49156
  443.5 3.7 copy-start.10
  443.5 3.7 copy-start.12
Sparse Core Ops, SparseCore 0:
  219.7 38.4 reduce-scatter.1
  290.0 33.1 all-gather.1
where the time goes:
time: 473 us; the launch traced here: 464 us
  waiting for transfers between devices  168 us (36%)
  blocking collectives  92.1 us (19%)
  matrix products  76.6 us (16%)
  local copies, waits for them, and re-layouts  47.4 us (10%)
  other arithmetic  46.7 us (10%)
  starting transfers between devices  18.9 us (4%)
  between operations  15.2 us (3%)
    dot_general x24, matrix products, product(): jnp.einsum(pattern, left_arr, right_arr, precision=lax.Precision.HIGHEST,...  76.6 us
    all_to_all x1, blocking collectives, body(): lax.all_to_all(adjoint, 'lat', split_axis=1, concat_axis=1, tiled=True)  64.2 us
    all_to_all x1, waiting for transfers between devices, body(): back = lax.all_to_all(back, 'lat', split_axis=1, concat_axis=1, tiled=True)  49 us
    all_to_all x1, waiting for transfers between devices, body(): lax.all_to_all(spectrum, 'lat', split_axis=1, concat_axis=1, tiled=True)  46.7 us
    reduce_scatter x1, waiting for transfers between devices, body(): lax.psum_scatter(2.0 * jnp.sum(columns_inverse_real(back), axis=0), 'dept...  38.5 us
    all_gather x1, waiting for transfers between devices, body(): res_spec = lax.all_gather(res_spec, 'depth', axis=2, tiled=True)  33.3 us
    all_to_all x1, blocking collectives, body(): lax.all_to_all(res_spec, 'lat', split_axis=1, concat_axis=1, tiled=True)  27.9 us
    sub x10, other arithmetic, rotate(): real_part * cos_table - imag_part * sin_table  25.5 us
  transfers between devices with their start and end apart: 4, of which 4 were waited for; matrix products, arithmetic and copies ran while one was open for 1% of the time, Pallas kernels for 0%

commit v1 on v0

v1 whole, which is shorter than its diff:
```python
import math

import jax
import jax.numpy as jnp
import ml_dtypes
import numpy as np
from jax import lax
from jax.experimental import pallas as pl
from jax.experimental.pallas import tpu as pltpu
from jax.sharding import PartitionSpec as P


TILE = 128
N = 4096
ROWS = 64
PLANES = 8
TWO_PI = 2.0 * math.pi
WAVE_RATIO = 0.266
DEPTH_SCALE = 0.001 / 5.32e-07
STEP_SIZE = 0.1
THRESHOLD = 0.25
F32 = jnp.float32
BF16 = jnp.bfloat16
VMEM_LIMIT = 48 * 1024 * 1024


def split_np(table):
    table = np.asarray(table, np.float64)
    high = table.astype(ml_dtypes.bfloat16)
    low = (table - high.astype(np.float64)).astype(ml_dtypes.bfloat16)
    return np.stack([high, low])


def twist_tables():
    k = np.arange(32)[:, None]
    b = np.arange(128)[None, :]
    angle = TWO_PI * ((k * b) % N) / N
    return np.cos(angle).astype(np.float32), np.sin(angle).astype(np.float32)


def matrix_forward():
    b = np.arange(128)
    angle = TWO_PI * ((b[:, None] * b[None, :]) % 128) / 128
    cos, sin = np.cos(angle), np.sin(angle)
    return np.block([[cos, -sin], [sin, cos]])


def matrix_inverse():
    return matrix_forward().T


def matrix_first_slot():
    b = np.arange(128)[:, None]
    m = np.arange(64)[None, :]
    low = TWO_PI * ((b * 32 * m) % N) / N
    high = TWO_PI * ((b * (16 + 32 * m)) % N) / N
    out = np.zeros((256, 256))
    out[:128, :64] = np.cos(low)
    out[:128, 128:192] = -np.sin(low)
    out[:128, 128] = 1.0 - 2.0 * (np.arange(128) % 2)
    out[128:, 64:128] = np.cos(high)
    out[128:, 192:] = -np.sin(high)
    return out


def matrix_first_slot_inverse():
    out = 2.0 * matrix_first_slot().T
    out[0] *= 0.5
    out[128] *= 0.5
    return out


def cosine_coefficients():
    nodes = 0.5 * math.pi**2 * (1.0 - np.cos(np.pi * (np.arange(64) + 0.5) / 64))
    fit = np.polynomial.chebyshev.Chebyshev.fit(nodes, np.cos(np.sqrt(nodes)), 8, domain=[0, math.pi**2])
    return [float(v) for v in fit.convert(kind=np.polynomial.Polynomial).coef]


COSINE = cosine_coefficients()
TURN_HIGH = float(np.float32(math.floor(TWO_PI * 4096) / 4096))
TURN_LOW = TWO_PI - TURN_HIGH


def turned(re, im, index, length, sign):
    index = index % length
    if index == 0:
        return re, im
    if 4 * index == length:
        if im is None:
            return None, (re if sign > 0 else -re)
        return (-im, re) if sign > 0 else (im, -re)
    c = math.cos(TWO_PI * index / length)
    s = sign * math.sin(TWO_PI * index / length)
    if im is None:
        return re * c, re * s
    if 8 * index == length:
        return ((re - im) * c, (re + im) * c) if sign > 0 else ((re + im) * c, (im - re) * c)
    if 8 * index == 3 * length:
        c = -c
        return (-((re + im) * c), (re - im) * c) if sign > 0 else ((im - re) * c, -((re + im) * c))
    return re * c - im * s, re * s + im * c


def plus(a, b):
    return b if a is None else (a if b is None else a + b)


def minus(a, b):
    if b is None:
        return a
    return -b if a is None else a - b


def real_forward(values):
    length = len(values)
    if length == 2:
        return [(values[0] + values[1], None), (values[0] - values[1], None)]
    even = real_forward(values[0::2])
    odd = real_forward(values[1::2])
    out = [None] * (length // 2 + 1)
    for k in range(length // 4 + 1):
        er, ei = even[k]
        tr, ti = turned(odd[k][0], odd[k][1], k, length, -1)
        out[k] = (plus(er, tr), plus(ei, ti))
        if 4 * k != length:
            out[length // 2 - k] = (minus(er, tr), minus(ti, ei))
    return out


def real_inverse(spectrum):
    length = 2 * (len(spectrum) - 1)
    if length == 2:
        return [spectrum[0][0] + spectrum[1][0], spectrum[0][0] - spectrum[1][0]]
    even, odd = [], []
    for k in range(length // 4 + 1):
        zr, zi = spectrum[k]
        yr, yi = spectrum[length // 2 - k]
        if 4 * k == length:
            even.append((zr + zr, None))
            odd.append((-(zi + zi), None))
            continue
        even.append((zr + yr, minus(zi, yi)))
        odd.append(turned(zr - yr, plus(zi, yi), k, length, 1))
    out = [None] * length
    out[0::2] = real_inverse(even)
    out[1::2] = real_inverse(odd)
    return out


def complex_sum(values, sign):
    length = len(values)
    if length == 1:
        return values
    even = complex_sum(values[0::2], sign)
    odd = complex_sum(values[1::2], sign)
    out = [None] * length
    for k in range(length // 2):
        er, ei = even[k]
        tr, ti = turned(odd[k][0], odd[k][1], k, length, sign)
        out[k] = (er + tr, ei + ti)
        out[k + length // 2] = (er - tr, ei - ti)
    return out


def parts(value):
    high = value.astype(BF16)
    return high, (value - high.astype(F32)).astype(BF16)


def mm(a, b, transposed=False):
    dims = (((1,), (1,)), ((), ())) if transposed else (((1,), (0,)), ((), ()))
    return lax.dot_general(a, b, dims, preferred_element_type=F32)


def lanes_of(shape):
    return lax.broadcasted_iota(jnp.int32, shape, len(shape) - 1)


def mark_tiles(tiles_ref, hits_ref, lat_place):
    for t in range(40):
        hits_ref[t] = 0.0
    for slot in range(16):
        hits_ref[tiles_ref[lat_place // 2, slot]] = 1.0


def rows_kernel(ids_ref, tiles_ref, depth_ref, vol_ref, holo_ref, tc_ref, ts_ref, wt_ref, out_ref, cur_ref, y_ref, hits_ref):
    depth_place, lat_place = ids_ref[0], ids_ref[1]
    mark_tiles(tiles_ref, hits_ref, lat_place)
    for a in range(32):
        cols = slice(a * TILE, (a + 1) * TILE)
        cur_ref[0:ROWS, cols] = vol_ref[:, cols].astype(F32) * hits_ref[a]
        cur_ref[ROWS:, cols] = holo_ref[:, cols].astype(F32)

    def group(g, carry):
        row = pl.multiple_of(g * 8, 8)
        base = (g // 8) * 1024 + (g % 8) * 8
        spec = real_forward([cur_ref[pl.ds(row, 8), a * TILE : (a + 1) * TILE] for a in range(32)])
        at = pl.ds(pl.multiple_of(base, 8), 8)
        y_ref[at, :128] = spec[0][0]
        y_ref[at, 128:] = spec[16][0]
        for k in range(1, 16):
            at = pl.ds(pl.multiple_of(base + k * ROWS, 8), 8)
            re, im = spec[k]
            c, s = tc_ref[k : k + 1, :], ts_ref[k : k + 1, :]
            y_ref[at, :128] = re * c + im * s
            y_ref[at, 128:] = im * c - re * s
        return carry

    lax.fori_loop(0, 16, group, 0)

    def apply(start, size, high, low):
        w_high, w_low = wt_ref[0, pl.ds(start, size), :], wt_ref[1, pl.ds(start, size), :]
        return mm(w_high, high, True) + (mm(w_high, low, True) + mm(w_low, high, True))

    for sg in range(4):
        high, low = parts(y_ref[sg * 256 : (sg + 1) * 256, :])
        o = apply(0, 256, high, low)
        for h in range(2):
            part = o[:, h * 128 : (h + 1) * 128]
            if sg == 0 and h == 0:
                first = apply(256, 256, high[:128], low[:128])
                part = jnp.where(lanes_of(part.shape) < ROWS, first, part)
            for c in range(2):
                out_ref[pl.ds(sg * 640 + c * 2 + h, 128, stride=5), :] = part[c * 128 : (c + 1) * 128]

    depth = depth_ref[0]
    half, slot_low = depth_place // 4, depth_place % 4
    for sg in range(4):
        slot = sg * 4 + slot_low
        y = y_ref[pl.ds(pl.multiple_of(1024 + slot * ROWS, ROWS), ROWS), :]
        high, low = parts(jnp.concatenate([y, y], axis=0))
        start = half * 128
        if sg == 0:
            start = start + jnp.where(slot_low == 0, 256, 0)
        o = apply(pl.multiple_of(start, 128), 128, high, low)
        out_ref[pl.ds(sg * 640 + 4, 128, stride=5), :] = jnp.where(lanes_of(o.shape) < ROWS, o, depth)


def signed(index):
    return jnp.where(index < N // 2, index, index - N)


def cosine(angle):
    turns = jnp.round(angle * (1.0 / TWO_PI))
    rest = (angle - turns * TURN_HIGH) - turns * TURN_LOW
    square = rest * rest
    value = COSINE[-1] * square + COSINE[-2]
    for coefficient in COSINE[-3::-1]:
        value = value * square + coefficient
    return value


def columns_kernel(ids_ref, in_ref, tc_ref, ts_ref, w_ref, wi_ref, out_ref, x_ref, z_ref, bend_ref):
    place = ids_ref[0] * ROWS + ids_ref[1]
    first = place == 0
    slot_group, col = place // 128, place % 128
    lane = lanes_of((8, 128))
    left = lane < ROWS
    fourth = lax.broadcasted_iota(jnp.int32, (8, 128), 0) % 4 == 0
    zero = jnp.zeros((8, 128), F32)

    def x_at(g, a, c):
        return pl.ds(pl.multiple_of(g * 512 + a * 16 + c * 8, 8), 8)

    ky = lax.broadcasted_iota(jnp.int32, (32, 128), 0) + 32 * lax.broadcasted_iota(jnp.int32, (32, 128), 1)
    uy = signed(ky).astype(F32) * (WAVE_RATIO / N)
    for g in range(5):
        if g == 4:
            kx = jnp.full((32, 128), -(N // 2), jnp.int32)
        else:
            slot = slot_group * 4 + g
            kx = slot + 32 * col
            if g == 0:
                kx = jnp.where(slot == 0, jnp.where(col < 64, 32 * col, 16 + 32 * (col - 64)), kx)
            kx = signed(jnp.full((32, 128), kx, jnp.int32))
        ux = kx.astype(F32) * (WAVE_RATIO / N)
        squared = uy * uy + ux * ux
        bend_ref[g * 32 : (g + 1) * 32, :] = squared / (1.0 + jnp.sqrt(1.0 - squared))

    depths = in_ref[pl.ds(4, 8, stride=320), :]
    scale = (TWO_PI * DEPTH_SCALE) * jnp.where(left, pltpu.roll(depths, 64, 1), depths)

    def gather(a, carry):
        start = a * 10
        for h in range(2):
            for c in range(2):
                lower = in_ref[pl.ds(start + c * 2 + h, 8, stride=320), :]
                upper = in_ref[pl.ds(start + 5 + c * 2 + h, 8, stride=320), :]
                one = jnp.where(left, lower, pltpu.roll(upper, 64, 1))
                two = jnp.where(left, pltpu.roll(lower, 64, 1), upper)
                if h == 0 and c == 1:
                    x_ref[x_at(5, a, 0), :] = jnp.where(first, one, zero)
                    x_ref[x_at(5, a, 1), :] = zero
                    one = jnp.where(first, zero, one)
                x_ref[x_at(2 * h, a, c), :] = one
                x_ref[x_at(2 * h + 1, a, c), :] = two
        lower = in_ref[pl.ds(start + 4, 8, stride=320), :]
        upper = in_ref[pl.ds(start + 9, 8, stride=320), :]
        both = jnp.where(left, lower, pltpu.roll(upper, 64, 1))
        x_ref[x_at(4, a, 0), :] = both
        x_ref[x_at(4, a, 1), :] = jnp.where(jnp.logical_and(first, fourth), zero, pltpu.roll(both, 4, 0))
        return carry

    lax.fori_loop(0, 32, gather, 0)

    def forward(g, carry):
        values = [(x_ref[x_at(g, a, 0), :], x_ref[x_at(g, a, 1), :]) for a in range(32)]
        for k, (re, im) in enumerate(complex_sum(values, -1)):
            at = pl.ds(pl.multiple_of(g * 256 + k * 8, 8), 8)
            if k > 0:
                c, s = tc_ref[k : k + 1, :], ts_ref[k : k + 1, :]
                re, im = re * c + im * s, im * c - re * s
            z_ref[at, :128] = re
            z_ref[at, 128:] = im
        return carry

    lax.fori_loop(0, 6, forward, 0)

    def product(g, table):
        at = slice(g * 256, (g + 1) * 256)
        high, low = parts(z_ref[at, :])
        z_ref[at, :] = mm(high, table[0]) + (mm(low, table[0]) + mm(high, table[1]))

    for g in range(6):
        product(g, w_ref)

    gain = STEP_SIZE * 2.0 / (N * N)

    def mix(k, carry):
        for index, (g, row) in enumerate(((0, 0), (1, 1), (2, 2), (3, 3), (5, 4))):
            at = pl.ds(pl.multiple_of(g * 256 + k * 8, 8), 8)
            wave = cosine(scale * bend_ref[pl.ds(index * 32 + k, 1), :])
            for half in (slice(0, 128), slice(128, 256)):
                total = jnp.sum(wave * z_ref[at, half], axis=0, keepdims=True)
                observed = z_ref[pl.ds(pl.multiple_of(1024 + k * 8, 8), 8), half]
                residual = observed[row : row + 1] - 2.0 * total
                z_ref[at, half] = (wave * gain) * residual
        return carry

    lax.fori_loop(0, 32, mix, 0)

    for g in (0, 1, 2, 3, 5):
        product(g, wi_ref)

    def backward(g, carry):
        g = jnp.where(g == 4, 5, g)
        values = []
        for k in range(32):
            at = pl.ds(pl.multiple_of(g * 256 + k * 8, 8), 8)
            re, im = z_ref[at, :128], z_ref[at, 128:]
            if k > 0:
                c, s = tc_ref[k : k + 1, :], ts_ref[k : k + 1, :]
                re, im = re * c - im * s, im * c + re * s
            values.append((re, im))
        for a, (re, im) in enumerate(complex_sum(values, 1)):
            x_ref[x_at(g, a, 0), :] = re
            x_ref[x_at(g, a, 1), :] = im
        return carry

    lax.fori_loop(0, 5, backward, 0)

    def scatter(a, carry):
        start = a * 8
        for h in range(2):
            for c in range(2):
                one = x_ref[x_at(2 * h, a, c), :]
                two = x_ref[x_at(2 * h + 1, a, c), :]
                if h == 0 and c == 1:
                    one = jnp.where(first, x_ref[x_at(5, a, 0), :], one)
                lower = jnp.where(left, one, pltpu.roll(two, 64, 1))
                upper = jnp.where(left, pltpu.roll(one, 64, 1), two)
                out_ref[pl.ds(start + c * 2 + h, 8, stride=256), :] = lower
                out_ref[pl.ds(start + 4 + c * 2 + h, 8, stride=256), :] = upper
        return carry

    lax.fori_loop(0, 32, scatter, 0)


def update_kernel(ids_ref, tiles_ref, vol_ref, in_ref, tc_ref, ts_ref, wi_ref, out_ref, y_ref, hits_ref):
    mark_tiles(tiles_ref, hits_ref, ids_ref[1])

    def apply(which, high, low):
        w_high, w_low = wi_ref[0, which], wi_ref[1, which]
        return mm(high, w_high) + (mm(low, w_high) + mm(high, w_low))

    for sg in range(4):
        for h in range(2):
            blocks = [in_ref[pl.ds(sg * 512 + c * 2 + h, 128, stride=4), :].T for c in range(2)]
            high, low = parts(jnp.concatenate(blocks, axis=1))
            slot = sg * 4 + h * 2
            if slot == 0:
                y_ref[0:64, :] = apply(1, high[:64], low[:64])
                y_ref[64:128, :] = apply(0, high[64:], low[64:])
            else:
                y_ref[slot * 64 : slot * 64 + 128, :] = apply(0, high, low)

    def group(g, carry):
        base = g * 8
        at = pl.ds(pl.multiple_of(base, 8), 8)
        spec = [(y_ref[at, :128], None)]
        for k in range(1, 16):
            at = pl.ds(pl.multiple_of(base + k * ROWS, 8), 8)
            re, im = y_ref[at, :128], y_ref[at, 128:]
            c, s = tc_ref[k : k + 1, :], ts_ref[k : k + 1, :]
            spec.append((re * c - im * s, im * c + re * s))
        at = pl.ds(pl.multiple_of(base, 8), 8)
        spec.append((y_ref[at, 128:], None))
        for a, value in enumerate(real_inverse(spec)):
            out_ref[at, a * TILE : (a + 1) * TILE] = value
        return carry

    lax.fori_loop(0, 8, group, 0)
    for a in range(32):
        cols = slice(a * TILE, (a + 1) * TILE)
        support = hits_ref[a]
        updated = vol_ref[:, cols].astype(F32) * support + out_ref[:, cols]
        out_ref[:, cols] = support * (updated - jnp.clip(updated, -THRESHOLD, THRESHOLD))


def call(kernel, out_shape, operands, scalars, scratch):
    specs = [pl.BlockSpec(memory_space=pltpu.SMEM if i < scalars else pltpu.VMEM) for i in range(len(operands))]
    return pl.pallas_call(
        kernel,
        out_shape=jax.ShapeDtypeStruct(out_shape, F32),
        in_specs=specs,
        out_specs=pl.BlockSpec(memory_space=pltpu.VMEM),
        scratch_shapes=scratch,
        compiler_params=pltpu.CompilerParams(vmem_limit_bytes=VMEM_LIMIT),
    )(*operands)


def rows_step(ids, tiles, depth, volume, hologram):
    tc, ts = twist_tables()
    wt = np.concatenate([matrix_forward().T, matrix_first_slot().T], axis=0)
    return call(
        rows_kernel,
        (2560, 128),
        (ids, tiles, depth, volume, hologram, tc, ts, split_np(wt)),
        3,
        [pltpu.VMEM((2 * ROWS, N), F32), pltpu.VMEM((2048, 256), F32), pltpu.SMEM((40,), F32)],
    )


def columns_step(ids, received):
    tc, ts = twist_tables()
    return call(
        columns_kernel,
        (2048, 128),
        (ids, received, tc, ts, split_np(matrix_forward()), split_np(matrix_inverse())),
        1,
        [pltpu.VMEM((3072, 128), F32), pltpu.VMEM((1536, 256), F32), pltpu.VMEM((160, 128), F32)],
    )


def update_step(ids, tiles, volume, received):
    tc, ts = twist_tables()
    wi = split_np(np.stack([matrix_inverse(), matrix_first_slot_inverse()]))
    return call(
        update_kernel,
        (ROWS, N),
        (ids, tiles, volume, received, tc, ts, wi),
        2,
        [pltpu.VMEM((1024, 256), F32), pltpu.SMEM((40,), F32)],
    )


def exchange(value, shape):
    moved = lax.all_to_all(value.reshape(shape), ("depth", "lat"), split_axis=0, concat_axis=0, tiled=True)
    return moved.reshape(value.shape)


def body(volume, hologram, plane_depth, tile_list):
    ids = jnp.stack([lax.axis_index("depth"), lax.axis_index("lat")]).astype(jnp.int32)
    tiles, volume = tile_list[0], volume[0]
    spectra = rows_step(ids, tiles, plane_depth, volume, hologram)
    spectra = exchange(spectra, (512, 1, 640))
    filtered = columns_step(ids, spectra)
    filtered = exchange(filtered, (512, 4, 128))
    return update_step(ids, tiles, volume, filtered)[None]


def solution(mesh):
    return jax.shard_map(
        body,
        mesh=mesh,
        in_specs=(P("depth", "lat", None), P("lat", None), P("depth"), P("depth", None, None)),
        out_specs=P("depth", "lat", None),
        check_vma=False,
    )
```

time: 473 us -> 128 us (0.27); the launches traced: 464 us -> 128 us
  waiting for transfers between devices: 168 us -> 0 us
  matrix products: 76.6 us -> 0 us
  other arithmetic: 46.7 us -> 0.07 us
  local copies, waits for them, and re-layouts: 47.4 us -> 5.37 us
  Pallas kernels: 0 us -> 19 us
  starting transfers between devices: 18.9 us -> 0 us
  between operations: 15.2 us -> 0.74 us
  blocking collectives: 92.1 us -> 103 us
    all_to_all x2 -> x0, waiting for transfers between devices: 95.6 us -> none  [the longest x1 49 us: body(): back = lax.all_to_all(back, 'lat', split_axis=1, concat_axis=1, tiled=True)]
    dot_general x24 -> x0, matrix products: 76.6 us -> none  [product(): jnp.einsum(pattern, left_arr, right_arr, precision=lax.Precision.HIGHEST,...]
    reduce_scatter x1 -> x0, waiting for transfers between devices: 38.5 us -> none  [body(): lax.psum_scatter(2.0 * jnp.sum(columns_inverse_real(back), axis=0), 'dept...]
    all_gather x1 -> x0, waiting for transfers between devices: 33.3 us -> none  [body(): res_spec = lax.all_gather(res_spec, 'depth', axis=2, tiled=True)]
    sub x15 -> x0, other arithmetic: 31 us -> none  [the longest x10 25.5 us: rotate(): real_part * cos_table - imag_part * sin_table]
    pallas_call x0 -> x3, Pallas kernels: none -> 19 us  [call(): pl.pallas_call(kernel, out_shape=jax.ShapeDtypeStruct(out_shape, F32), in...]
    all_to_all x2 -> x0, starting transfers between devices: 18.6 us -> none  [the longest x1 11.6 us: body(): lax.all_to_all(spectrum, 'lat', split_axis=1, concat_axis=1, tiled=True)]
    all_to_all x2, blocking collectives: 92.1 us -> 103 us  [exchange(): lax.all_to_all(value.reshape(shape), ('depth', 'lat'), split_axis=0, conc...]
  transfers between devices with their start and end apart: 4 -> 0, of which waited for: 4 -> 0; matrix products, arithmetic and copies ran while one was open for 1% -> 0% of each run, Pallas kernels for 0% -> 0%
where the time goes in v1:
time: 128 us
  blocking collectives  103 us (80%)
  Pallas kernels  19 us (15%)
  local copies, waits for them, and re-layouts  5.37 us (4%)
    all_to_all x2, blocking collectives, exchange(): lax.all_to_all(value.reshape(shape), ('depth', 'lat'), split_axis=0, conc...  103 us
    pallas_call x3, Pallas kernels, call(): pl.pallas_call(kernel, out_shape=jax.ShapeDtypeStruct(out_shape, F32), in...  19 us
    unnamed x23, local copies, waits for them, and re-layouts  5.37 us

profile of v1, /device:TPU:1, one launch (start us, length us, event | category | flops | bytes accessed | tf_op | source)
XLA Modules:
  0.0 127.8 jit_solution(15163066701387455738)
XLA Ops:
  0.7 0.8 copy.16
  1.4 0.1 pad_add_fusion.ids_ref
  1.5 0.0 copy-start
  1.5 1.0 copy-done
  2.5 0.0 copy-start.2
  2.5 1.0 copy-done.2
  3.6 0.0 copy-start.4
  3.6 1.0 copy-done.4
  4.6 0.0 copy-start.7
  4.6 0.7 copy-done.7
  5.3 0.0 copy-start.9
  5.3 0.7 copy-done.9
  6.1 2.7 %shard_map.136 = f32[2560,128]{1,0:T(8,128)S(1)} custom-call(s32[2]{0:T(128)S(1)} %pad_add_fusion.ids_ref, s32[32,16]{1,0:T(8,128)S(1)} %bitcast.15, f32[1]{0:T(128)S(6)} %copy.18.depth_ref, bf16[64,4096]{1,0:T(8,128)(2,1)S(1)} %bitcast.13, bf16[64,4096]{1,0:T(8,128)(2,1)S(1)} %copy-done.2, f32[32,128]{1,0:T(8,128)S(1)} %copy-done.9, ...), custom_call_target="tpu_custom_call" | custom-call | tf_op jit(solution)/shard_map/pallas_call | solution.py:422
  8.8 0.0 copy-start.5
  8.8 0.0 copy-start.6
  8.8 0.0 copy-start.8
  8.8 0.0 copy-start.10
  8.8 59.6 %all_to_all.10 = f32[512,1,640]{2,1,0:T(1,128)S(1)} all-to-all(f32[512,1,640]{2,1,0:T(1,128)S(1)} %bitcast.10), channel_id=1, replica_groups=mesh['depth'=8,'lat'=64] {'depth','lat'}, dimensions={0} | all-to-all | bytes 2621440 | tf_op jit(solution)/shard_map/all_to_all | solution.py:468
  68.4 0.0 copy-done.5
  68.4 0.0 copy-done.6
  68.4 0.0 copy-done.8
  68.4 0.0 copy-done.10
  68.4 13.1 %shard_map.137 = f32[2048,128]{1,0:T(8,128)S(1)} custom-call(s32[2]{0:T(128)S(1)} %pad_add_fusion.ids_ref, f32[2560,128]{1,0:T(8,128)S(1)} %bitcast.9, f32[32,128]{1,0:T(8,128)S(1)} %copy-done.10, f32[32,128]{1,0:T(8,128)S(1)} %copy-done.8, bf16[2,256,256]{2,1,0:T(8,128)(2,1)S(1)} %copy-done.6, bf16[2,256,256]{2,1,0:T(8,128)(2,1)S(1)} %copy-done.5), custom_call_target="tpu_custom_call" | custom-call | tf_op jit(solution)/shard_map/pallas_call | solution.py:422
  81.5 0.0 copy-start.1
  81.5 0.0 copy-start.3
  81.6 43.1 %all_to_all.11 = f32[512,4,128]{2,1,0:T(4,128)S(1)} all-to-all(f32[512,4,128]{2,1,0:T(4,128)S(1)} %bitcast.11), channel_id=1, replica_groups=mesh['depth'=8,'lat'=64] {'depth','lat'}, dimensions={0} | all-to-all | bytes 2097152 | tf_op jit(solution)/shard_map/all_to_all | solution.py:468
  124.7 0.0 copy-done.1
  124.7 0.0 copy-done.3
  124.7 3.1 %shard_map.138 = f32[64,4096]{1,0:T(8,128)} custom-call(s32[2]{0:T(128)S(1)} %pad_add_fusion.ids_ref, s32[32,16]{1,0:T(8,128)S(1)} %bitcast.16, bf16[64,4096]{1,0:T(8,128)(2,1)S(1)} %bitcast.14, f32[2048,128]{1,0:T(8,128)S(1)} %bitcast.12, f32[32,128]{1,0:T(8,128)S(1)} %copy-done.10, f32[32,128]{1,0:T(8,128)S(1)} %copy-done.8, ...), custom_call_target="tpu_custom_call" | custom-call | tf_op jit(solution)/shard_map/pallas_call | solution.py:422
Async XLA Ops:
  1.5 1.0 copy-start
  2.5 1.0 copy-start.2
  3.6 1.0 copy-start.4
  4.6 0.7 copy-start.7
  5.3 0.7 copy-start.9
  8.8 59.6 %copy-start.5 = (bf16[2,256,256]{2,1,0:T(8,128)(2,1)S(1)}, bf16[2,256,256]{2,1,0:T(8,128)(2,1)}, u32[]{:S(2)}) copy-start(bf16[2,256,256]{2,1,0:T(8,128)(2,1)} %constant.25.clone.wi_ref) | copy-start | bytes 786436
  8.8 59.6 %copy-start.6 = (bf16[2,256,256]{2,1,0:T(8,128)(2,1)S(1)}, bf16[2,256,256]{2,1,0:T(8,128)(2,1)}, u32[]{:S(2)}) copy-start(bf16[2,256,256]{2,1,0:T(8,128)(2,1)} %constant.24.clone.w_ref) | copy-start | bytes 786436
  8.8 59.6 %copy-start.8 = (f32[32,128]{1,0:T(8,128)S(1)}, f32[32,128]{1,0:T(8,128)}, u32[]{:S(2)}) copy-start(f32[32,128]{1,0:T(8,128)} %constant.22.clone.ts_ref) | copy-start | bytes 49156
  8.8 59.6 %copy-start.10 = (f32[32,128]{1,0:T(8,128)S(1)}, f32[32,128]{1,0:T(8,128)}, u32[]{:S(2)}) copy-start(f32[32,128]{1,0:T(8,128)} %constant.21.clone.tc_ref) | copy-start | bytes 49156
  81.5 43.2 %copy-start.1 = (bf16[1,64,4096]{2,1,0:T(8,128)(2,1)S(1)}, bf16[1,64,4096]{2,1,0:T(8,128)(2,1)}, u32[]{:S(2)}) copy-start(bf16[1,64,4096]{2,1,0:T(8,128)(2,1)} %param.14) | copy-start | bytes 1572868
  81.5 43.2 %copy-start.3 = (bf16[2,2,256,256]{3,2,1,0:T(8,128)(2,1)S(1)}, bf16[2,2,256,256]{3,2,1,0:T(8,128)(2,1)}, u32[]{:S(2)}) copy-start(bf16[2,2,256,256]{3,2,1,0:T(8,128)(2,1)} %constant.26.clone.wi_ref) | copy-start | bytes 1572868

commit v2 on v1

--- a/solution.py
+++ b/solution.py
@@ -22,6 +22,7 @@
 F32 = jnp.float32
 BF16 = jnp.bfloat16
 VMEM_LIMIT = 48 * 1024 * 1024
+PRODUCT_ROWS = 512
 
 
 def split_np(table):
@@ -180,33 +181,46 @@
     for t in range(40):
         hits_ref[t] = 0.0
     for slot in range(16):
-        hits_ref[tiles_ref[lat_place // 2, slot]] = 1.0
-
-
-def rows_kernel(ids_ref, tiles_ref, depth_ref, vol_ref, holo_ref, tc_ref, ts_ref, wt_ref, out_ref, cur_ref, y_ref, hits_ref):
+        hits_ref[tiles_ref[slot, lat_place // 2]] = 1.0
+
+
+def rows_kernel(ids_ref, tiles_ref, depth_ref, vol_ref, holo_ref, tw_ref, wt_hbm, out_ref, src_ref, tw, wt_ref, y_ref, hits_ref, sems):
+    copies = [
+        pltpu.make_async_copy(vol_ref, src_ref.at[0:ROWS], sems.at[0]),
+        pltpu.make_async_copy(holo_ref, src_ref.at[ROWS : 2 * ROWS], sems.at[1]),
+        pltpu.make_async_copy(tw_ref, tw, sems.at[2]),
+        pltpu.make_async_copy(wt_hbm, wt_ref, sems.at[3]),
+    ]
+    for copy in copies:
+        copy.start()
     depth_place, lat_place = ids_ref[0], ids_ref[1]
     mark_tiles(tiles_ref, hits_ref, lat_place)
     for a in range(32):
-        cols = slice(a * TILE, (a + 1) * TILE)
-        cur_ref[0:ROWS, cols] = vol_ref[:, cols].astype(F32) * hits_ref[a]
-        cur_ref[ROWS:, cols] = holo_ref[:, cols].astype(F32)
+        hits_ref[40 + a] = 1.0
+    for copy in copies[:3]:
+        copy.wait()
 
     def group(g, carry):
-        row = pl.multiple_of(g * 8, 8)
-        base = (g // 8) * 1024 + (g % 8) * 8
-        spec = real_forward([cur_ref[pl.ds(row, 8), a * TILE : (a + 1) * TILE] for a in range(32)])
-        at = pl.ds(pl.multiple_of(base, 8), 8)
+        which = g // 4
+        values = []
+        for a in range(32):
+            tile = src_ref[pl.ds(pl.multiple_of(g * 16, 16), 16), a * TILE : (a + 1) * TILE]
+            values.append(tile.astype(F32) * hits_ref[which * 40 + a])
+        base = which * 1024 + (g % 4) * 16
+        spec = real_forward(values)
+        at = pl.ds(pl.multiple_of(base, 16), 16)
         y_ref[at, :128] = spec[0][0]
         y_ref[at, 128:] = spec[16][0]
         for k in range(1, 16):
-            at = pl.ds(pl.multiple_of(base + k * ROWS, 8), 8)
+            at = pl.ds(pl.multiple_of(base + k * ROWS, 16), 16)
             re, im = spec[k]
-            c, s = tc_ref[k : k + 1, :], ts_ref[k : k + 1, :]
+            c, s = tw[k : k + 1, :], tw[32 + k : 33 + k, :]
             y_ref[at, :128] = re * c + im * s
             y_ref[at, 128:] = im * c - re * s
         return carry
 
-    lax.fori_loop(0, 16, group, 0)
+    lax.fori_loop(0, 8, group, 0)
+    copies[3].wait()
 
     def apply(start, size, high, low):
         w_high, w_low = wt_ref[0, pl.ds(start, size), :], wt_ref[1, pl.ds(start, size), :]
@@ -250,17 +264,30 @@
     return value
 
 
-def columns_kernel(ids_ref, in_ref, tc_ref, ts_ref, w_ref, wi_ref, out_ref, x_ref, z_ref, bend_ref):
-    place = ids_ref[0] * ROWS + ids_ref[1]
+def columns_kernel(ids_ref, in_ref, tc_ref, ts_ref, w_ref, wi_ref, out_ref, x_ref, zr_ref, zi_ref, bend_ref):
+    place = ids_ref[1] * PLANES + ids_ref[0]
     first = place == 0
     slot_group, col = place // 128, place % 128
-    lane = lanes_of((8, 128))
-    left = lane < ROWS
+    left = lanes_of((8, 128)) < ROWS
     fourth = lax.broadcasted_iota(jnp.int32, (8, 128), 0) % 4 == 0
     zero = jnp.zeros((8, 128), F32)
 
+    def swap(value):
+        return pltpu.roll(value, ROWS, 1)
+
     def x_at(g, a, c):
         return pl.ds(pl.multiple_of(g * 512 + a * 16 + c * 8, 8), 8)
+
+    def received(a, upper, q):
+        return in_ref[pl.ds(a * 80 + upper * 40 + q, 8, stride=5), :]
+
+    def store_spectrum(g, k, re, im):
+        if k > 0:
+            c, s = tc_ref[k : k + 1, :], ts_ref[k : k + 1, :]
+            re, im = re * c + im * s, im * c - re * s
+        at = pl.ds(g * 320 + k, 8, stride=40)
+        zr_ref[at, :] = re
+        zi_ref[at, :] = im
 
     ky = lax.broadcasted_iota(jnp.int32, (32, 128), 0) + 32 * lax.broadcasted_iota(jnp.int32, (32, 128), 1)
     uy = signed(ky).astype(F32) * (WAVE_RATIO / N)
@@ -277,103 +304,111 @@
         squared = uy * uy + ux * ux
         bend_ref[g * 32 : (g + 1) * 32, :] = squared / (1.0 + jnp.sqrt(1.0 - squared))
 
-    depths = in_ref[pl.ds(4, 8, stride=320), :]
-    scale = (TWO_PI * DEPTH_SCALE) * jnp.where(left, pltpu.roll(depths, 64, 1), depths)
+    def forward(h, carry):
+        packed = jnp.logical_and(jnp.logical_and(first, h == 0), left)
+        halves = []
+        for upper in range(2):
+            values = []
+            for a in range(32):
+                re, im = received(a, upper, h), received(a, upper, 2 + h)
+                values.append((re, jnp.where(packed, zero, im)))
+            halves.append(complex_sum(values, -1))
+        for k in range(32):
+            lower, upper = halves[0][k], halves[1][k]
+            store_spectrum(2 * h, k, *[jnp.where(left, p, swap(q)) for p, q in zip(lower, upper)])
+            store_spectrum(2 * h + 1, k, *[jnp.where(left, swap(p), q) for p, q in zip(lower, upper)])
+        return carry
+
+    lax.fori_loop(0, 2, forward, 0)
 
     def gather(a, carry):
-        start = a * 10
-        for h in range(2):
-            for c in range(2):
-                lower = in_ref[pl.ds(start + c * 2 + h, 8, stride=320), :]
-                upper = in_ref[pl.ds(start + 5 + c * 2 + h, 8, stride=320), :]
-                one = jnp.where(left, lower, pltpu.roll(upper, 64, 1))
-                two = jnp.where(left, pltpu.roll(lower, 64, 1), upper)
-                if h == 0 and c == 1:
-                    x_ref[x_at(5, a, 0), :] = jnp.where(first, one, zero)
-                    x_ref[x_at(5, a, 1), :] = zero
-                    one = jnp.where(first, zero, one)
-                x_ref[x_at(2 * h, a, c), :] = one
-                x_ref[x_at(2 * h + 1, a, c), :] = two
-        lower = in_ref[pl.ds(start + 4, 8, stride=320), :]
-        upper = in_ref[pl.ds(start + 9, 8, stride=320), :]
-        both = jnp.where(left, lower, pltpu.roll(upper, 64, 1))
-        x_ref[x_at(4, a, 0), :] = both
-        x_ref[x_at(4, a, 1), :] = jnp.where(jnp.logical_and(first, fourth), zero, pltpu.roll(both, 4, 0))
-        return carry
-
-    lax.fori_loop(0, 32, gather, 0)
-
-    def forward(g, carry):
+        both = jnp.where(left, received(a, 0, 4), swap(received(a, 1, 4)))
+        x_ref[x_at(0, a, 0), :] = both
+        x_ref[x_at(0, a, 1), :] = jnp.where(jnp.logical_and(first, fourth), zero, pltpu.roll(both, 4, 0))
+        both = jnp.where(left, received(a, 0, 2), swap(received(a, 1, 2)))
+        x_ref[x_at(1, a, 0), :] = jnp.where(first, both, zero)
+        x_ref[x_at(1, a, 1), :] = zero
+        return carry
+
+    lax.fori_loop(0, 32, gather, 0, unroll=8)
+
+    def forward_extra(g, carry):
         values = [(x_ref[x_at(g, a, 0), :], x_ref[x_at(g, a, 1), :]) for a in range(32)]
         for k, (re, im) in enumerate(complex_sum(values, -1)):
-            at = pl.ds(pl.multiple_of(g * 256 + k * 8, 8), 8)
-            if k > 0:
-                c, s = tc_ref[k : k + 1, :], ts_ref[k : k + 1, :]
-                re, im = re * c + im * s, im * c - re * s
-            z_ref[at, :128] = re
-            z_ref[at, 128:] = im
-        return carry
-
-    lax.fori_loop(0, 6, forward, 0)
-
-    def product(g, table):
-        at = slice(g * 256, (g + 1) * 256)
-        high, low = parts(z_ref[at, :])
-        z_ref[at, :] = mm(high, table[0]) + (mm(low, table[0]) + mm(high, table[1]))
-
-    for g in range(6):
-        product(g, w_ref)
-
+            store_spectrum(4 + g, k, re, im)
+        return carry
+
+    lax.fori_loop(0, 2, forward_extra, 0)
+
+    def product(start, size, table):
+        slabs = [slice((r // 32) * 40, (r // 32) * 40 + 32) for r in range(start, start + size, 32)]
+        pairs = [parts(jnp.concatenate([ref[at, :] for at in slabs], axis=0)) for ref in (zr_ref, zi_ref)]
+        high = jnp.concatenate([pairs[0][0], pairs[1][0]], axis=1)
+        low = jnp.concatenate([pairs[0][1], pairs[1][1]], axis=1)
+        value = mm(high, table[0]) + (mm(low, table[0]) + mm(high, table[1]))
+        for i, at in enumerate(slabs):
+            zr_ref[at, :] = value[i * 32 : (i + 1) * 32, :128]
+            zi_ref[at, :] = value[i * 32 : (i + 1) * 32, 128:]
+
+    for start in range(0, 1536, PRODUCT_ROWS):
+        product(start, PRODUCT_ROWS, w_ref)
+
+    scales = []
+    for p in range(PLANES):
+        row = jnp.broadcast_to(in_ref[p * 5 + 4 : p * 5 + 5, :], (8, 128))
+        scales.append((TWO_PI * DEPTH_SCALE) * jnp.where(left, swap(row), row))
     gain = STEP_SIZE * 2.0 / (N * N)
 
-    def mix(k, carry):
-        for index, (g, row) in enumerate(((0, 0), (1, 1), (2, 2), (3, 3), (5, 4))):
-            at = pl.ds(pl.multiple_of(g * 256 + k * 8, 8), 8)
-            wave = cosine(scale * bend_ref[pl.ds(index * 32 + k, 1), :])
-            for half in (slice(0, 128), slice(128, 256)):
-                total = jnp.sum(wave * z_ref[at, half], axis=0, keepdims=True)
-                observed = z_ref[pl.ds(pl.multiple_of(1024 + k * 8, 8), 8), half]
-                residual = observed[row : row + 1] - 2.0 * total
-                z_ref[at, half] = (wave * gain) * residual
-        return carry
-
-    lax.fori_loop(0, 32, mix, 0)
-
-    for g in (0, 1, 2, 3, 5):
-        product(g, wi_ref)
-
-    def backward(g, carry):
-        g = jnp.where(g == 4, 5, g)
-        values = []
+    def mix(j, carry):
+        extra = None
+        for index, g in ((4, 5), (0, 0), (1, 1), (2, 2), (3, 3)):
+            bend = bend_ref[pl.ds(pl.multiple_of(index * 32 + j * 8, 8), 8), :]
+            waves = [cosine(scale * bend) for scale in scales]
+            rows = [pl.ds(pl.multiple_of(g * 320 + p * 40 + j * 8, 8), 8) for p in range(PLANES)]
+            at = pl.ds(pl.multiple_of(1280 + index * 40 + j * 8, 8), 8)
+            scaled = []
+            for ref in (zr_ref, zi_ref):
+                terms = [wave * ref[row, :] for wave, row in zip(waves, rows)]
+                while len(terms) > 1:
+                    terms = [p + q for p, q in zip(terms[0::2], terms[1::2])]
+                scaled.append((ref[at, :] - 2.0 * terms[0]) * gain)
+            if index == 4:
+                extra = [jnp.where(first, value, zero) for value in scaled], waves
+                continue
+            for p, row in enumerate(rows):
+                re, im = waves[p] * scaled[0], waves[p] * scaled[1]
+                if index == 0:
+                    re = re - extra[1][p] * extra[0][1]
+                    im = im + extra[1][p] * extra[0][0]
+                zr_ref[row, :] = re
+                zi_ref[row, :] = im
+        return carry
+
+    lax.fori_loop(0, 4, mix, 0)
+
+    for start in range(0, 1024, PRODUCT_ROWS):
+        product(start, PRODUCT_ROWS, wi_ref)
+
+    def backward(h, carry):
+        lower, upper = [], []
         for k in range(32):
-            at = pl.ds(pl.multiple_of(g * 256 + k * 8, 8), 8)
-            re, im = z_ref[at, :128], z_ref[at, 128:]
-            if k > 0:
-                c, s = tc_ref[k : k + 1, :], ts_ref[k : k + 1, :]
-                re, im = re * c - im * s, im * c + re * s
-            values.append((re, im))
-        for a, (re, im) in enumerate(complex_sum(values, 1)):
-            x_ref[x_at(g, a, 0), :] = re
-            x_ref[x_at(g, a, 1), :] = im
-        return carry
-
-    lax.fori_loop(0, 5, backward, 0)
-
-    def scatter(a, carry):
-        start = a * 8
-        for h in range(2):
-            for c in range(2):
-                one = x_ref[x_at(2 * h, a, c), :]
-                two = x_ref[x_at(2 * h + 1, a, c), :]
-                if h == 0 and c == 1:
-                    one = jnp.where(first, x_ref[x_at(5, a, 0), :], one)
-                lower = jnp.where(left, one, pltpu.roll(two, 64, 1))
-                upper = jnp.where(left, pltpu.roll(one, 64, 1), two)
-                out_ref[pl.ds(start + c * 2 + h, 8, stride=256), :] = lower
-                out_ref[pl.ds(start + 4 + c * 2 + h, 8, stride=256), :] = upper
-        return carry
-
-    lax.fori_loop(0, 32, scatter, 0)
+            columns = []
+            for g in (2 * h, 2 * h + 1):
+                at = pl.ds(g * 320 + k, 8, stride=40)
+                re, im = zr_ref[at, :], zi_ref[at, :]
+                if k > 0:
+                    c, s = tc_ref[k : k + 1, :], ts_ref[k : k + 1, :]
+                    re, im = re * c - im * s, im * c + re * s
+                columns.append((re, im))
+            lower.append(tuple(jnp.where(left, p, swap(q)) for p, q in zip(*columns)))
+            upper.append(tuple(jnp.where(left, swap(p), q) for p, q in zip(*columns)))
+        for number, values in enumerate((lower, upper)):
+            for a, (re, im) in enumerate(complex_sum(values, 1)):
+                out_ref[pl.ds(a * 64 + number * 32 + h, 8, stride=4), :] = re
+                out_ref[pl.ds(a * 64 + number * 32 + 2 + h, 8, stride=4), :] = im
+        return carry
+
+    lax.fori_loop(0, 2, backward, 0)
 
 
 def update_kernel(ids_ref, tiles_ref, vol_ref, in_ref, tc_ref, ts_ref, wi_ref, out_ref, y_ref, hits_ref):
@@ -417,12 +452,12 @@
         out_ref[:, cols] = support * (updated - jnp.clip(updated, -THRESHOLD, THRESHOLD))
 
 
-def call(kernel, out_shape, operands, scalars, scratch):
-    specs = [pl.BlockSpec(memory_space=pltpu.SMEM if i < scalars else pltpu.VMEM) for i in range(len(operands))]
+def call(kernel, out_shape, operands, places, scratch):
+    spaces = {"s": pltpu.SMEM, "v": pltpu.VMEM, "h": pltpu.HBM}
     return pl.pallas_call(
         kernel,
         out_shape=jax.ShapeDtypeStruct(out_shape, F32),
-        in_specs=specs,
+        in_specs=[pl.BlockSpec(memory_space=spaces[place]) for place in places],
         out_specs=pl.BlockSpec(memory_space=pltpu.VMEM),
         scratch_shapes=scratch,
         compiler_params=pltpu.CompilerParams(vmem_limit_bytes=VMEM_LIMIT),
@@ -430,14 +465,20 @@
 
 
 def rows_step(ids, tiles, depth, volume, hologram):
-    tc, ts = twist_tables()
     wt = np.concatenate([matrix_forward().T, matrix_first_slot().T], axis=0)
     return call(
         rows_kernel,
         (2560, 128),
-        (ids, tiles, depth, volume, hologram, tc, ts, split_np(wt)),
-        3,
-        [pltpu.VMEM((2 * ROWS, N), F32), pltpu.VMEM((2048, 256), F32), pltpu.SMEM((40,), F32)],
+        (ids, tiles, depth, volume, hologram, np.concatenate(twist_tables()), split_np(wt)),
+        "ssshhhh",
+        [
+            pltpu.VMEM((2 * ROWS, N), BF16),
+            pltpu.VMEM((64, 128), F32),
+            pltpu.VMEM((2, 512, 256), BF16),
+            pltpu.VMEM((2048, 256), F32),
+            pltpu.SMEM((80,), F32),
+            pltpu.SemaphoreType.DMA((4,)),
+        ],
     )
 
 
@@ -447,8 +488,13 @@
         columns_kernel,
         (2048, 128),
         (ids, received, tc, ts, split_np(matrix_forward()), split_np(matrix_inverse())),
-        1,
-        [pltpu.VMEM((3072, 128), F32), pltpu.VMEM((1536, 256), F32), pltpu.VMEM((160, 128), F32)],
+        "svvvvv",
+        [
+            pltpu.VMEM((1024, 128), F32),
+            pltpu.VMEM((1920, 128), F32),
+            pltpu.VMEM((1920, 128), F32),
+            pltpu.VMEM((160, 128), F32),
+        ],
     )
 
 
@@ -459,19 +505,19 @@
         update_kernel,
         (ROWS, N),
         (ids, tiles, volume, received, tc, ts, wi),
-        2,
+        "ssvvvvv",
         [pltpu.VMEM((1024, 256), F32), pltpu.SMEM((40,), F32)],
     )
 
 
 def exchange(value, shape):
-    moved = lax.all_to_all(value.reshape(shape), ("depth", "lat"), split_axis=0, concat_axis=0, tiled=True)
+    moved = lax.all_to_all(value.reshape(shape), ("lat", "depth"), split_axis=0, concat_axis=0, tiled=True)
     return moved.reshape(value.shape)
 
 
 def body(volume, hologram, plane_depth, tile_list):
     ids = jnp.stack([lax.axis_index("depth"), lax.axis_index("lat")]).astype(jnp.int32)
-    tiles, volume = tile_list[0], volume[0]
+    tiles, volume = tile_list[0].T, volume[0]
     spectra = rows_step(ids, tiles, plane_depth, volume, hologram)
     spectra = exchange(spectra, (512, 1, 640))
     filtered = columns_step(ids, spectra)

time: 128 us -> 119 us (0.930)
  Pallas kernels: 19 us -> 10.5 us
    pallas_call x3, Pallas kernels: 19 us -> 10.5 us  [call(): pl.pallas_call(kernel, out_shape=jax.ShapeDtypeStruct(out_shape, F32), in...]
    unnamed x23 -> x24, local copies, waits for them, and re-layouts: 5.37 us -> 4.62 us
where the time goes in v2:
time: 119 us
  blocking collectives  103 us (87%)
  Pallas kernels  10.5 us (9%)
  local copies, waits for them, and re-layouts  4.62 us (4%)
    all_to_all x2, blocking collectives, exchange(): lax.all_to_all(value.reshape(shape), ('lat', 'depth'), split_axis=0, conc...  103 us
    pallas_call x3, Pallas kernels, call(): pl.pallas_call(kernel, out_shape=jax.ShapeDtypeStruct(out_shape, F32), in...  10.5 us
    unnamed x24, local copies, waits for them, and re-layouts  4.62 us

profile of v2, /device:TPU:1, one launch (start us, length us, event | category | flops | bytes accessed | tf_op | source)
XLA Modules:
  0.0 118.6 jit_solution(15967862552808431286)
XLA Ops:
  0.7 0.1 pad_add_fusion.ids_ref
  0.7 0.0 copy-start
  0.7 1.0 copy-done
  1.8 0.0 copy-start.2
  1.8 1.0 copy-done.2
  2.8 0.0 copy-start.4
  2.8 1.0 copy-done.4
  3.9 0.0 copy-start.9
  3.9 0.8 copy-done.9
  4.6 0.0 copy-start.10
  4.6 0.7 copy-done.10
  5.3 2.9 %shard_map.127 = f32[2560,128]{1,0:T(8,128)S(1)} custom-call(s32[2]{0:T(128)S(1)} %pad_add_fusion.ids_ref, s32[16,32]{1,0:T(8,128)S(1)} %bitcast.17, f32[1]{0:T(128)S(6)} %copy.15.depth_ref, bf16[64,4096]{1,0:T(8,128)(2,1)S(1)} %bitcast.15, bf16[64,4096]{1,0:T(8,128)(2,1)S(1)} %copy-done.2, f32[64,128]{1,0:T(8,128)S(1)} %copy-done.9, ...), custom_call_target="tpu_custom_call" | custom-call | tf_op jit(solution)/shard_map/pallas_call | solution.py:457
  8.2 0.0 copy-start.5
  8.2 0.0 copy-start.6
  8.2 0.0 copy-start.7
  8.2 0.0 copy-start.8
  8.3 60.1 %all_to_all.10 = f32[512,1,640]{2,1,0:T(1,128)S(1)} all-to-all(f32[512,1,640]{2,1,0:T(1,128)S(1)} %bitcast.11), channel_id=1, replica_groups=mesh['depth'=8,'lat'=64] {'lat','depth'}, dimensions={0} | all-to-all | bytes 2621440 | tf_op jit(solution)/shard_map/all_to_all | solution.py:514
  68.4 0.0 copy-done.5
  68.4 0.0 copy-done.6
  68.4 0.0 copy-done.7
  68.4 0.0 copy-done.8
  68.4 4.7 %shard_map.128 = f32[2048,128]{1,0:T(8,128)S(1)} custom-call(s32[2]{0:T(128)S(1)} %pad_add_fusion.ids_ref, f32[2560,128]{1,0:T(8,128)S(1)} %bitcast.12, f32[32,128]{1,0:T(8,128)S(1)} %copy-done.8, f32[32,128]{1,0:T(8,128)S(1)} %copy-done.7, bf16[2,256,256]{2,1,0:T(8,128)(2,1)S(1)} %copy-done.6, bf16[2,256,256]{2,1,0:T(8,128)(2,1)S(1)} %copy-done.5), custom_call_target="tpu_custom_call" | custom-call | tf_op jit(solution)/shard_map/pallas_call | solution.py:457
  73.1 0.0 copy-start.1
  73.1 0.0 copy-start.3
  73.1 0.0 copy-start.11
  73.1 42.4 %all_to_all.11 = f32[512,4,128]{2,1,0:T(4,128)S(1)} all-to-all(f32[512,4,128]{2,1,0:T(4,128)S(1)} %bitcast.13), channel_id=1, replica_groups=mesh['depth'=8,'lat'=64] {'lat','depth'}, dimensions={0} | all-to-all | bytes 2097152 | tf_op jit(solution)/shard_map/all_to_all | solution.py:514
  115.5 0.0 copy-done.1
  115.6 0.0 copy-done.3
  115.6 0.0 copy-done.11
  115.6 3.0 %shard_map.129 = f32[64,4096]{1,0:T(8,128)} custom-call(s32[2]{0:T(128)S(1)} %pad_add_fusion.ids_ref, s32[16,32]{1,0:T(8,128)S(1)} %bitcast.18, bf16[64,4096]{1,0:T(8,128)(2,1)S(1)} %bitcast.16, f32[2048,128]{1,0:T(8,128)S(1)} %bitcast.14, f32[32,128]{1,0:T(8,128)S(1)} %copy-done.8, f32[32,128]{1,0:T(8,128)S(1)} %copy-done.7, ...), custom_call_target="tpu_custom_call" | custom-call | tf_op jit(solution)/shard_map/pallas_call | solution.py:457
Async XLA Ops:
  0.7 1.0 copy-start
  1.8 1.0 copy-start.2
  2.8 1.0 copy-start.4
  3.9 0.8 copy-start.9
  4.6 0.7 copy-start.10
  8.2 60.2 %copy-start.5 = (bf16[2,256,256]{2,1,0:T(8,128)(2,1)S(1)}, bf16[2,256,256]{2,1,0:T(8,128)(2,1)}, u32[]{:S(2)}) copy-start(bf16[2,256,256]{2,1,0:T(8,128)(2,1)} %constant.28.clone.wi_ref) | copy-start | bytes 786436
  8.2 60.2 %copy-start.6 = (bf16[2,256,256]{2,1,0:T(8,128)(2,1)S(1)}, bf16[2,256,256]{2,1,0:T(8,128)(2,1)}, u32[]{:S(2)}) copy-start(bf16[2,256,256]{2,1,0:T(8,128)(2,1)} %constant.27.clone.w_ref) | copy-start | bytes 786436
  8.2 60.2 %copy-start.7 = (f32[32,128]{1,0:T(8,128)S(1)}, f32[32,128]{1,0:T(8,128)}, u32[]{:S(2)}) copy-start(f32[32,128]{1,0:T(8,128)} %constant.26.clone.ts_ref) | copy-start | bytes 49156
  8.2 60.2 %copy-start.8 = (f32[32,128]{1,0:T(8,128)S(1)}, f32[32,128]{1,0:T(8,128)}, u32[]{:S(2)}) copy-start(f32[32,128]{1,0:T(8,128)} %constant.25.clone.tc_ref) | copy-start | bytes 49156
  73.1 42.5 %copy-start.1 = (bf16[1,64,4096]{2,1,0:T(8,128)(2,1)S(1)}, bf16[1,64,4096]{2,1,0:T(8,128)(2,1)}, u32[]{:S(2)}) copy-start(bf16[1,64,4096]{2,1,0:T(8,128)(2,1)} %param.13) | copy-start | bytes 1572868
  73.1 42.5 %copy-start.3 = (bf16[2,2,256,256]{3,2,1,0:T(8,128)(2,1)S(1)}, bf16[2,2,256,256]{3,2,1,0:T(8,128)(2,1)}, u32[]{:S(2)}) copy-start(bf16[2,2,256,256]{3,2,1,0:T(8,128)(2,1)} %constant.29.clone.wi_ref) | copy-start | bytes 1572868
  73.1 42.4 %copy-start.11 = (s32[1,32,16]{1,2,0:T(8,128)S(1)}, s32[1,32,16]{1,2,0:T(8,128)}, u32[]{:S(2)}) copy-start(s32[1,32,16]{1,2,0:T(8,128)} %param.16) | copy-start | bytes 6148

commit v3 on v2

--- a/solution.py
+++ b/solution.py
@@ -177,6 +177,10 @@
     return lax.broadcasted_iota(jnp.int32, shape, len(shape) - 1)
 
 
+def places():
+    return lax.axis_index("depth"), lax.axis_index("lat")
+
+
 def mark_tiles(tiles_ref, hits_ref, lat_place):
     for t in range(40):
         hits_ref[t] = 0.0
@@ -184,20 +188,24 @@
         hits_ref[tiles_ref[slot, lat_place // 2]] = 1.0
 
 
-def rows_kernel(ids_ref, tiles_ref, depth_ref, vol_ref, holo_ref, tw_ref, wt_hbm, out_ref, src_ref, tw, wt_ref, y_ref, hits_ref, sems):
+def rows_kernel(
+    depth_ref, tiles_hbm, vol_hbm, holo_hbm, tw_hbm, wt_hbm, out_ref, tiles_ref, src_ref, tw, wt_ref, y_ref, hits_ref, sems
+):
     copies = [
-        pltpu.make_async_copy(vol_ref, src_ref.at[0:ROWS], sems.at[0]),
-        pltpu.make_async_copy(holo_ref, src_ref.at[ROWS : 2 * ROWS], sems.at[1]),
-        pltpu.make_async_copy(tw_ref, tw, sems.at[2]),
+        pltpu.make_async_copy(tiles_hbm, tiles_ref, sems.at[4]),
+        pltpu.make_async_copy(vol_hbm, src_ref.at[0:ROWS], sems.at[0]),
+        pltpu.make_async_copy(holo_hbm, src_ref.at[ROWS : 2 * ROWS], sems.at[1]),
+        pltpu.make_async_copy(tw_hbm, tw, sems.at[2]),
         pltpu.make_async_copy(wt_hbm, wt_ref, sems.at[3]),
     ]
     for copy in copies:
         copy.start()
-    depth_place, lat_place = ids_ref[0], ids_ref[1]
-    mark_tiles(tiles_ref, hits_ref, lat_place)
+    depth_place, lat_place = places()
     for a in range(32):
         hits_ref[40 + a] = 1.0
-    for copy in copies[:3]:
+    copies[0].wait()
+    mark_tiles(tiles_ref, hits_ref, lat_place)
+    for copy in copies[1:4]:
         copy.wait()
 
     def group(g, carry):
@@ -220,7 +228,7 @@
         return carry
 
     lax.fori_loop(0, 8, group, 0)
-    copies[3].wait()
+    copies[4].wait()
 
     def apply(start, size, high, low):
         w_high, w_low = wt_ref[0, pl.ds(start, size), :], wt_ref[1, pl.ds(start, size), :]
@@ -264,8 +272,9 @@
     return value
 
 
-def columns_kernel(ids_ref, in_ref, tc_ref, ts_ref, w_ref, wi_ref, out_ref, x_ref, zr_ref, zi_ref, bend_ref):
-    place = ids_ref[1] * PLANES + ids_ref[0]
+def columns_kernel(in_ref, tc_ref, ts_ref, w_ref, wi_ref, out_ref, x_ref, zr_ref, zi_ref, bend_ref):
+    depth_place, lat_place = places()
+    place = lat_place * PLANES + depth_place
     first = place == 0
     slot_group, col = place // 128, place % 128
     left = lanes_of((8, 128)) < ROWS
@@ -411,8 +420,8 @@
     lax.fori_loop(0, 2, backward, 0)
 
 
-def update_kernel(ids_ref, tiles_ref, vol_ref, in_ref, tc_ref, ts_ref, wi_ref, out_ref, y_ref, hits_ref):
-    mark_tiles(tiles_ref, hits_ref, ids_ref[1])
+def update_kernel(tiles_ref, vol_ref, in_ref, tc_ref, ts_ref, wi_ref, out_ref, y_ref, hits_ref):
+    mark_tiles(tiles_ref, hits_ref, places()[1])
 
     def apply(which, high, low):
         w_high, w_low = wi_ref[0, which], wi_ref[1, which]
@@ -454,6 +463,9 @@
 
 def call(kernel, out_shape, operands, places, scratch):
     spaces = {"s": pltpu.SMEM, "v": pltpu.VMEM, "h": pltpu.HBM}
+    operands = [
+        pltpu.with_memory_space_constraint(x, pltpu.HBM) if place == "h" else x for x, place in zip(operands, places)
+    ]
     return pl.pallas_call(
         kernel,
         out_shape=jax.ShapeDtypeStruct(out_shape, F32),
@@ -464,31 +476,32 @@
     )(*operands)
 
 
-def rows_step(ids, tiles, depth, volume, hologram):
+def rows_step(tiles, depth, volume, hologram):
     wt = np.concatenate([matrix_forward().T, matrix_first_slot().T], axis=0)
     return call(
         rows_kernel,
         (2560, 128),
-        (ids, tiles, depth, volume, hologram, np.concatenate(twist_tables()), split_np(wt)),
-        "ssshhhh",
+        (depth, tiles, volume, hologram, np.concatenate(twist_tables()), split_np(wt)),
+        "shhhhh",
         [
+            pltpu.SMEM((16, 32), jnp.int32),
             pltpu.VMEM((2 * ROWS, N), BF16),
             pltpu.VMEM((64, 128), F32),
             pltpu.VMEM((2, 512, 256), BF16),
             pltpu.VMEM((2048, 256), F32),
             pltpu.SMEM((80,), F32),
-            pltpu.SemaphoreType.DMA((4,)),
+            pltpu.SemaphoreType.DMA((5,)),
         ],
     )
 
 
-def columns_step(ids, received):
+def columns_step(received):
     tc, ts = twist_tables()
     return call(
         columns_kernel,
         (2048, 128),
-        (ids, received, tc, ts, split_np(matrix_forward()), split_np(matrix_inverse())),
-        "svvvvv",
+        (received, tc, ts, split_np(matrix_forward()), split_np(matrix_inverse())),
+        "vvvvv",
         [
             pltpu.VMEM((1024, 128), F32),
             pltpu.VMEM((1920, 128), F32),
@@ -498,14 +511,14 @@
     )
 
 
-def update_step(ids, tiles, volume, received):
+def update_step(tiles, volume, received):
     tc, ts = twist_tables()
     wi = split_np(np.stack([matrix_inverse(), matrix_first_slot_inverse()]))
     return call(
         update_kernel,
         (ROWS, N),
-        (ids, tiles, volume, received, tc, ts, wi),
-        "ssvvvvv",
+        (tiles, volume, received, tc, ts, wi),
+        "svvvvv",
         [pltpu.VMEM((1024, 256), F32), pltpu.SMEM((40,), F32)],
     )
 
@@ -516,13 +529,12 @@
 
 
 def body(volume, hologram, plane_depth, tile_list):
-    ids = jnp.stack([lax.axis_index("depth"), lax.axis_index("lat")]).astype(jnp.int32)
     tiles, volume = tile_list[0].T, volume[0]
-    spectra = rows_step(ids, tiles, plane_depth, volume, hologram)
+    spectra = rows_step(tiles, plane_depth, volume, hologram)
     spectra = exchange(spectra, (512, 1, 640))
-    filtered = columns_step(ids, spectra)
+    filtered = columns_step(spectra)
     filtered = exchange(filtered, (512, 4, 128))
-    return update_step(ids, tiles, volume, filtered)[None]
+    return update_step(tiles, volume, filtered)[None]
 
 
 def solution(mesh):

time: 119 us -> 114 us (0.958)
  local copies, waits for them, and re-layouts: 4.62 us -> 0.05 us
    unnamed x24 -> x14, local copies, waits for them, and re-layouts: 4.62 us -> 0.05 us
where the time goes in v3:
time: 114 us
  blocking collectives  103 us (90%)
  Pallas kernels  10.3 us (9%)
    all_to_all x2, blocking collectives, exchange(): lax.all_to_all(value.reshape(shape), ('lat', 'depth'), split_axis=0, conc...  103 us
    pallas_call x3, Pallas kernels, call(): pl.pallas_call(kernel, out_shape=jax.ShapeDtypeStruct(out_shape, F32), in...  10.3 us

profile of v3, /device:TPU:1, one launch (start us, length us, event | category | flops | bytes accessed | tf_op | source)
XLA Modules:
  0.0 113.7 jit_solution(5102599541174287442)
XLA Ops:
  0.7 3.2 %shard_map.127 = f32[2560,128]{1,0:T(8,128)S(1)} custom-call(f32[1]{0:T(128)S(6)} %copy.15.depth_ref, s32[16,32]{1,0:T(8,128)} %bitcast.15, bf16[64,4096]{1,0:T(8,128)(2,1)} %bitcast.13, bf16[64,4096]{1,0:T(8,128)(2,1)} %holo_hbm.1, f32[64,128]{1,0:T(8,128)} %constant.14.clone.tw_hbm, bf16[2,512,256]{2,1,0:T(8,128)(2,1)} %constant.15.clone.wt_hbm), custom_call_target="tpu_custom_call" | custom-call | tf_op jit(solution)/shard_map/pallas_call | solution.py:469
  3.9 0.0 copy-start.2
  3.9 0.0 copy-start.3
  3.9 0.0 copy-start.4
  3.9 0.0 copy-start.5
  3.9 60.1 %all_to_all.10 = f32[512,1,640]{2,1,0:T(1,128)S(1)} all-to-all(f32[512,1,640]{2,1,0:T(1,128)S(1)} %bitcast.9), channel_id=1, replica_groups=mesh['depth'=8,'lat'=64] {'lat','depth'}, dimensions={0} | all-to-all | bytes 2621440 | tf_op jit(solution)/shard_map/all_to_all | solution.py:527
  64.1 0.0 copy-done.2
  64.1 0.0 copy-done.3
  64.1 0.0 copy-done.4
  64.1 0.0 copy-done.5
  64.1 4.1 %shard_map.128 = f32[2048,128]{1,0:T(8,128)S(1)} custom-call(f32[2560,128]{1,0:T(8,128)S(1)} %bitcast.10, f32[32,128]{1,0:T(8,128)S(1)} %copy-done.5, f32[32,128]{1,0:T(8,128)S(1)} %copy-done.4, bf16[2,256,256]{2,1,0:T(8,128)(2,1)S(1)} %copy-done.3, bf16[2,256,256]{2,1,0:T(8,128)(2,1)S(1)} %copy-done.2), custom_call_target="tpu_custom_call" | custom-call | tf_op jit(solution)/shard_map/pallas_call | solution.py:469
  68.2 0.0 copy-start
  68.2 0.0 copy-start.1
  68.2 0.0 copy-start.6
  68.2 42.4 %all_to_all.11 = f32[512,4,128]{2,1,0:T(4,128)S(1)} all-to-all(f32[512,4,128]{2,1,0:T(4,128)S(1)} %bitcast.12), channel_id=1, replica_groups=mesh['depth'=8,'lat'=64] {'lat','depth'}, dimensions={0} | all-to-all | bytes 2097152 | tf_op jit(solution)/shard_map/all_to_all | solution.py:527
  110.7 0.0 copy-done
  110.7 0.0 copy-done.1
  110.7 0.0 copy-done.6
  110.7 3.0 %shard_map.129 = f32[64,4096]{1,0:T(8,128)} custom-call(s32[16,32]{1,0:T(8,128)S(1)} %bitcast.16, bf16[64,4096]{1,0:T(8,128)(2,1)S(1)} %bitcast.14, f32[2048,128]{1,0:T(8,128)S(1)} %bitcast.11, f32[32,128]{1,0:T(8,128)S(1)} %copy-done.5, f32[32,128]{1,0:T(8,128)S(1)} %copy-done.4, bf16[2,2,256,256]{3,2,1,0:T(8,128)(2,1)S(1)} %copy-done.1), custom_call_target="tpu_custom_call" | custom-call | tf_op jit(solution)/shard_map/pallas_call | solution.py:469
Async XLA Ops:
  3.9 60.2 %copy-start.2 = (bf16[2,256,256]{2,1,0:T(8,128)(2,1)S(1)}, bf16[2,256,256]{2,1,0:T(8,128)(2,1)}, u32[]{:S(2)}) copy-start(bf16[2,256,256]{2,1,0:T(8,128)(2,1)} %constant.19.clone.wi_ref) | copy-start | bytes 786436
  3.9 60.2 %copy-start.3 = (bf16[2,256,256]{2,1,0:T(8,128)(2,1)S(1)}, bf16[2,256,256]{2,1,0:T(8,128)(2,1)}, u32[]{:S(2)}) copy-start(bf16[2,256,256]{2,1,0:T(8,128)(2,1)} %constant.18.clone.w_ref) | copy-start | bytes 786436
  3.9 60.2 %copy-start.4 = (f32[32,128]{1,0:T(8,128)S(1)}, f32[32,128]{1,0:T(8,128)}, u32[]{:S(2)}) copy-start(f32[32,128]{1,0:T(8,128)} %constant.17.clone.ts_ref) | copy-start | bytes 49156
  3.9 60.2 %copy-start.5 = (f32[32,128]{1,0:T(8,128)S(1)}, f32[32,128]{1,0:T(8,128)}, u32[]{:S(2)}) copy-start(f32[32,128]{1,0:T(8,128)} %constant.16.clone.tc_ref) | copy-start | bytes 49156
  68.2 42.5 %copy-start = (bf16[1,64,4096]{2,1,0:T(8,128)(2,1)S(1)}, bf16[1,64,4096]{2,1,0:T(8,128)(2,1)}, u32[]{:S(2)}) copy-start(bf16[1,64,4096]{2,1,0:T(8,128)(2,1)} %param.13) | copy-start | bytes 1572868
  68.2 42.5 %copy-start.1 = (bf16[2,2,256,256]{3,2,1,0:T(8,128)(2,1)S(1)}, bf16[2,2,256,256]{3,2,1,0:T(8,128)(2,1)}, u32[]{:S(2)}) copy-start(bf16[2,2,256,256]{3,2,1,0:T(8,128)(2,1)} %constant.20.clone.wi_ref) | copy-start | bytes 1572868
  68.2 42.4 %copy-start.6 = (s32[1,32,16]{1,2,0:T(8,128)S(1)}, s32[1,32,16]{1,2,0:T(8,128)}, u32[]{:S(2)}) copy-start(s32[1,32,16]{1,2,0:T(8,128)} %param.16) | copy-start | bytes 6148

commit v4 on v3

--- a/solution.py
+++ b/solution.py
@@ -1,3 +1,4 @@
+import functools
 import math
 
 import jax
@@ -72,14 +73,13 @@
 
 
 def cosine_coefficients():
-    nodes = 0.5 * math.pi**2 * (1.0 - np.cos(np.pi * (np.arange(64) + 0.5) / 64))
-    fit = np.polynomial.chebyshev.Chebyshev.fit(nodes, np.cos(np.sqrt(nodes)), 8, domain=[0, math.pi**2])
+    nodes = 0.125 * (1.0 - np.cos(np.pi * (np.arange(64) + 0.5) / 64))
+    values = np.cos(TWO_PI * np.sqrt(nodes))
+    fit = np.polynomial.chebyshev.Chebyshev.fit(nodes, values, 6, domain=[0.0, 0.25])
     return [float(v) for v in fit.convert(kind=np.polynomial.Polynomial).coef]
 
 
 COSINE = cosine_coefficients()
-TURN_HIGH = float(np.float32(math.floor(TWO_PI * 4096) / 4096))
-TURN_LOW = TWO_PI - TURN_HIGH
 
 
 def turned(re, im, index, length, sign):
@@ -189,32 +189,30 @@
 
 
 def rows_kernel(
-    depth_ref, tiles_hbm, vol_hbm, holo_hbm, tw_hbm, wt_hbm, out_ref, tiles_ref, src_ref, tw, wt_ref, y_ref, hits_ref, sems
+    depth_ref, tiles_hbm, vol_hbm, holo_hbm, tw_hbm, wt_hbm, out_ref, mask_ref, tiles_ref, src_ref, tw, wt_ref, y_ref, hits_ref, sems
 ):
     copies = [
-        pltpu.make_async_copy(tiles_hbm, tiles_ref, sems.at[4]),
-        pltpu.make_async_copy(vol_hbm, src_ref.at[0:ROWS], sems.at[0]),
-        pltpu.make_async_copy(holo_hbm, src_ref.at[ROWS : 2 * ROWS], sems.at[1]),
+        pltpu.make_async_copy(tiles_hbm, tiles_ref, sems.at[0]),
+        pltpu.make_async_copy(vol_hbm, src_ref.at[0:ROWS], sems.at[1]),
         pltpu.make_async_copy(tw_hbm, tw, sems.at[2]),
-        pltpu.make_async_copy(wt_hbm, wt_ref, sems.at[3]),
+        pltpu.make_async_copy(holo_hbm, src_ref.at[ROWS : 2 * ROWS], sems.at[3]),
+        pltpu.make_async_copy(wt_hbm, wt_ref, sems.at[4]),
     ]
     for copy in copies:
         copy.start()
     depth_place, lat_place = places()
-    for a in range(32):
-        hits_ref[40 + a] = 1.0
     copies[0].wait()
     mark_tiles(tiles_ref, hits_ref, lat_place)
-    for copy in copies[1:4]:
-        copy.wait()
-
-    def group(g, carry):
-        which = g // 4
+    for a in range(32):
+        mask_ref[a : a + 1, :] = jnp.full((1, 128), hits_ref[a], F32)
+
+    def group(masked, g, carry):
+        rows = pl.ds(pl.multiple_of(g * 16 + (0 if masked else ROWS), 16), 16)
         values = []
         for a in range(32):
-            tile = src_ref[pl.ds(pl.multiple_of(g * 16, 16), 16), a * TILE : (a + 1) * TILE]
-            values.append(tile.astype(F32) * hits_ref[which * 40 + a])
-        base = which * 1024 + (g % 4) * 16
+            tile = src_ref[rows, a * TILE : (a + 1) * TILE].astype(F32)
+            values.append(tile * mask_ref[a : a + 1, :] if masked else tile)
+        base = g * 16 + (0 if masked else 1024)
         spec = real_forward(values)
         at = pl.ds(pl.multiple_of(base, 16), 16)
         y_ref[at, :128] = spec[0][0]
@@ -227,7 +225,11 @@
             y_ref[at, 128:] = im * c - re * s
         return carry
 
-    lax.fori_loop(0, 8, group, 0)
+    copies[1].wait()
+    copies[2].wait()
+    lax.fori_loop(0, 4, functools.partial(group, True), 0)
+    copies[3].wait()
+    lax.fori_loop(0, 4, functools.partial(group, False), 0)
     copies[4].wait()
 
     def apply(start, size, high, low):
@@ -262,9 +264,8 @@
     return jnp.where(index < N // 2, index, index - N)
 
 
-def cosine(angle):
-    turns = jnp.round(angle * (1.0 / TWO_PI))
-    rest = (angle - turns * TURN_HIGH) - turns * TURN_LOW
+def cosine(turns):
+    rest = turns - jnp.round(turns)
     square = rest * rest
     value = COSINE[-1] * square + COSINE[-2]
     for coefficient in COSINE[-3::-1]:
@@ -283,6 +284,10 @@
 
     def swap(value):
         return pltpu.roll(value, ROWS, 1)
+
+    def exchanged(p, q):
+        middle = swap(jnp.where(left, q, p))
+        return jnp.where(left, p, middle), jnp.where(left, middle, q)
 
     def x_at(g, a, c):
         return pl.ds(pl.multiple_of(g * 512 + a * 16 + c * 8, 8), 8)
@@ -324,8 +329,8 @@
             halves.append(complex_sum(values, -1))
         for k in range(32):
             lower, upper = halves[0][k], halves[1][k]
-            store_spectrum(2 * h, k, *[jnp.where(left, p, swap(q)) for p, q in zip(lower, upper)])
-            store_spectrum(2 * h + 1, k, *[jnp.where(left, swap(p), q) for p, q in zip(lower, upper)])
+            for number, column in enumerate(zip(*[exchanged(p, q) for p, q in zip(lower, upper)])):
+                store_spectrum(2 * h + number, k, *column)
         return carry
 
     lax.fori_loop(0, 2, forward, 0)
@@ -365,7 +370,7 @@
     scales = []
     for p in range(PLANES):
         row = jnp.broadcast_to(in_ref[p * 5 + 4 : p * 5 + 5, :], (8, 128))
-        scales.append((TWO_PI * DEPTH_SCALE) * jnp.where(left, swap(row), row))
+        scales.append(DEPTH_SCALE * jnp.where(left, swap(row), row))
     gain = STEP_SIZE * 2.0 / (N * N)
 
     def mix(j, carry):
@@ -409,8 +414,9 @@
                     c, s = tc_ref[k : k + 1, :], ts_ref[k : k + 1, :]
                     re, im = re * c - im * s, im * c + re * s
                 columns.append((re, im))
-            lower.append(tuple(jnp.where(left, p, swap(q)) for p, q in zip(*columns)))
-            upper.append(tuple(jnp.where(left, swap(p), q) for p, q in zip(*columns)))
+            halves = list(zip(*[exchanged(p, q) for p, q in zip(*columns)]))
+            lower.append(halves[0])
+            upper.append(halves[1])
         for number, values in enumerate((lower, upper)):
             for a, (re, im) in enumerate(complex_sum(values, 1)):
                 out_ref[pl.ds(a * 64 + number * 32 + h, 8, stride=4), :] = re
@@ -420,9 +426,7 @@
     lax.fori_loop(0, 2, backward, 0)
 
 
-def update_kernel(tiles_ref, vol_ref, in_ref, tc_ref, ts_ref, wi_ref, out_ref, y_ref, hits_ref):
-    mark_tiles(tiles_ref, hits_ref, places()[1])
-
+def update_kernel(mask_ref, vol_ref, in_ref, tc_ref, ts_ref, wi_ref, out_hbm, y_ref, new_ref, sems):
     def apply(which, high, low):
         w_high, w_low = wi_ref[0, which], wi_ref[1, which]
         return mm(high, w_high) + (mm(low, w_high) + mm(high, w_low))
@@ -438,39 +442,43 @@
             else:
                 y_ref[slot * 64 : slot * 64 + 128, :] = apply(0, high, low)
 
+    def copy_out(g):
+        rows = pl.ds(pl.multiple_of(g * 16, 16), 16)
+        return pltpu.make_async_copy(new_ref.at[rows], out_hbm.at[rows], sems.at[g])
+
     def group(g, carry):
-        base = g * 8
-        at = pl.ds(pl.multiple_of(base, 8), 8)
-        spec = [(y_ref[at, :128], None)]
+        rows = pl.ds(pl.multiple_of(g * 16, 16), 16)
+        spec = [(y_ref[rows, :128], None)]
         for k in range(1, 16):
-            at = pl.ds(pl.multiple_of(base + k * ROWS, 8), 8)
+            at = pl.ds(pl.multiple_of(g * 16 + k * ROWS, 16), 16)
             re, im = y_ref[at, :128], y_ref[at, 128:]
             c, s = tc_ref[k : k + 1, :], ts_ref[k : k + 1, :]
             spec.append((re * c - im * s, im * c + re * s))
-        at = pl.ds(pl.multiple_of(base, 8), 8)
-        spec.append((y_ref[at, 128:], None))
-        for a, value in enumerate(real_inverse(spec)):
-            out_ref[at, a * TILE : (a + 1) * TILE] = value
-        return carry
-
-    lax.fori_loop(0, 8, group, 0)
-    for a in range(32):
-        cols = slice(a * TILE, (a + 1) * TILE)
-        support = hits_ref[a]
-        updated = vol_ref[:, cols].astype(F32) * support + out_ref[:, cols]
-        out_ref[:, cols] = support * (updated - jnp.clip(updated, -THRESHOLD, THRESHOLD))
-
-
-def call(kernel, out_shape, operands, places, scratch):
+        spec.append((y_ref[rows, 128:], None))
+        for a, step in enumerate(real_inverse(spec)):
+            cols = slice(a * TILE, (a + 1) * TILE)
+            support = mask_ref[a : a + 1, :]
+            updated = vol_ref[rows, cols].astype(F32) * support + step
+            new_ref[rows, cols] = support * (updated - jnp.clip(updated, -THRESHOLD, THRESHOLD))
+        copy_out(g).start()
+        return carry
+
+    lax.fori_loop(0, 4, group, 0)
+    for g in range(4):
+        copy_out(g).wait()
+
+
+def call(kernel, out_shapes, operands, places, scratch):
     spaces = {"s": pltpu.SMEM, "v": pltpu.VMEM, "h": pltpu.HBM}
+    specs = [pl.BlockSpec(memory_space=spaces[place]) for place in places]
     operands = [
         pltpu.with_memory_space_constraint(x, pltpu.HBM) if place == "h" else x for x, place in zip(operands, places)
     ]
     return pl.pallas_call(
         kernel,
-        out_shape=jax.ShapeDtypeStruct(out_shape, F32),
-        in_specs=[pl.BlockSpec(memory_space=spaces[place]) for place in places],
-        out_specs=pl.BlockSpec(memory_space=pltpu.VMEM),
+        out_shape=[jax.ShapeDtypeStruct(shape, F32) for shape in out_shapes],
+        in_specs=specs[: len(operands)],
+        out_specs=specs[len(operands) :],
         scratch_shapes=scratch,
         compiler_params=pltpu.CompilerParams(vmem_limit_bytes=VMEM_LIMIT),
     )(*operands)
@@ -480,16 +488,16 @@
     wt = np.concatenate([matrix_forward().T, matrix_first_slot().T], axis=0)
     return call(
         rows_kernel,
-        (2560, 128),
+        [(2560, 128), (32, 128)],
         (depth, tiles, volume, hologram, np.concatenate(twist_tables()), split_np(wt)),
-        "shhhhh",
+        "shhhhhvv",
         [
             pltpu.SMEM((16, 32), jnp.int32),
             pltpu.VMEM((2 * ROWS, N), BF16),
             pltpu.VMEM((64, 128), F32),
             pltpu.VMEM((2, 512, 256), BF16),
             pltpu.VMEM((2048, 256), F32),
-            pltpu.SMEM((80,), F32),
+            pltpu.SMEM((40,), F32),
             pltpu.SemaphoreType.DMA((5,)),
         ],
     )
@@ -499,9 +507,9 @@
     tc, ts = twist_tables()
     return call(
         columns_kernel,
-        (2048, 128),
+        [(2048, 128)],
         (received, tc, ts, split_np(matrix_forward()), split_np(matrix_inverse())),
-        "vvvvv",
+        "vvvvvv",
         [
             pltpu.VMEM((1024, 128), F32),
             pltpu.VMEM((1920, 128), F32),
@@ -511,15 +519,15 @@
     )
 
 
-def update_step(tiles, volume, received):
+def update_step(mask, volume, received):
     tc, ts = twist_tables()
     wi = split_np(np.stack([matrix_inverse(), matrix_first_slot_inverse()]))
     return call(
         update_kernel,
-        (ROWS, N),
-        (tiles, volume, received, tc, ts, wi),
-        "svvvvv",
-        [pltpu.VMEM((1024, 256), F32), pltpu.SMEM((40,), F32)],
+        [(ROWS, N)],
+        (mask, volume, received, tc, ts, wi),
+        "vvvvvvh",
+        [pltpu.VMEM((1024, 256), F32), pltpu.VMEM((ROWS, N), F32), pltpu.SemaphoreType.DMA((4,))],
     )
 
 
@@ -530,11 +538,12 @@
 
 def body(volume, hologram, plane_depth, tile_list):
     tiles, volume = tile_list[0].T, volume[0]
-    spectra = rows_step(tiles, plane_depth, volume, hologram)
+    spectra, mask = rows_step(tiles, plane_depth, volume, hologram)
     spectra = exchange(spectra, (512, 1, 640))
-    filtered = columns_step(spectra)
+    (filtered,) = columns_step(spectra)
     filtered = exchange(filtered, (512, 4, 128))
-    return update_step(tiles, volume, filtered)[None]
+    (updated,) = update_step(mask, volume, filtered)
+    return updated[None]
 
 
 def solution(mesh):

time: 114 us -> 112 us (0.982)
  Pallas kernels: 10.3 us -> 8.79 us
    pallas_call x3, Pallas kernels: 10.3 us -> 8.79 us  [call(): pl.pallas_call(kernel, out_shape=[jax.ShapeDtypeStruct(shape, F32) for sh...]
where the time goes in v4:
time: 112 us
  blocking collectives  103 us (92%)
  Pallas kernels  8.79 us (8%)
    all_to_all x2, blocking collectives, exchange(): lax.all_to_all(value.reshape(shape), ('lat', 'depth'), split_axis=0, conc...  103 us
    pallas_call x3, Pallas kernels, call(): pl.pallas_call(kernel, out_shape=[jax.ShapeDtypeStruct(shape, F32) for sh...  8.79 us

profile of v4, /device:TPU:1, one launch (start us, length us, event | category | flops | bytes accessed | tf_op | source)
XLA Modules:
  0.0 112.1 jit_solution(9202739554197479051)
XLA Ops:
  0.7 2.9 %shard_map.127 = (f32[2560,128]{1,0:T(8,128)S(1)}, f32[32,128]{1,0:T(8,128)S(1)}) custom-call(f32[1]{0:T(128)S(6)} %copy.15.depth_ref, s32[16,32]{1,0:T(8,128)} %bitcast.15, bf16[64,4096]{1,0:T(8,128)(2,1)} %bitcast.12, bf16[64,4096]{1,0:T(8,128)(2,1)} %holo_hbm.1, f32[64,128]{1,0:T(8,128)} %constant.14.clone.tw_hbm, bf16[2,512,256]{2,1,0:T(8,128)(2,1)} %constant.15.clone.wt_hbm), custom_call_target="tpu_custom_call" | custom-call | tf_op jit(solution)/shard_map/pallas_call | solution.py:477
  3.6 0.0 copy-start.2
  3.6 0.0 copy-start.3
  3.6 0.0 copy-start.4
  3.6 0.0 copy-start.5
  3.6 60.1 %all_to_all.10 = f32[512,1,640]{2,1,0:T(1,128)S(1)} all-to-all(f32[512,1,640]{2,1,0:T(1,128)S(1)} %bitcast.14), channel_id=1, replica_groups=mesh['depth'=8,'lat'=64] {'lat','depth'}, dimensions={0} | all-to-all | bytes 2621440 | tf_op jit(solution)/shard_map/all_to_all | solution.py:535
  63.8 0.0 copy-done.2
  63.8 0.0 copy-done.3
  63.8 0.0 copy-done.4
  63.8 0.0 copy-done.5
  63.8 3.8 %shard_map.128 = f32[2048,128]{1,0:T(8,128)S(1)} custom-call(f32[2560,128]{1,0:T(8,128)S(1)} %bitcast.9, f32[32,128]{1,0:T(8,128)S(1)} %copy-done.5, f32[32,128]{1,0:T(8,128)S(1)} %copy-done.4, bf16[2,256,256]{2,1,0:T(8,128)(2,1)S(1)} %copy-done.3, bf16[2,256,256]{2,1,0:T(8,128)(2,1)S(1)} %copy-done.2), custom_call_target="tpu_custom_call" | custom-call | tf_op jit(solution)/shard_map/pallas_call | solution.py:477
  67.6 0.0 copy-start
  67.6 0.0 copy-start.1
  67.6 42.4 %all_to_all.11 = f32[512,4,128]{2,1,0:T(4,128)S(1)} all-to-all(f32[512,4,128]{2,1,0:T(4,128)S(1)} %bitcast.11), channel_id=1, replica_groups=mesh['depth'=8,'lat'=64] {'lat','depth'}, dimensions={0} | all-to-all | bytes 2097152 | tf_op jit(solution)/shard_map/all_to_all | solution.py:535
  110.1 0.0 copy-done
  110.1 0.0 copy-done.1
  110.1 2.1 %shard_map.129 = f32[64,4096]{1,0:T(8,128)} custom-call(f32[32,128]{1,0:T(8,128)S(1)} %get-tuple-element.7.mask_ref, bf16[64,4096]{1,0:T(8,128)(2,1)S(1)} %bitcast.13, f32[2048,128]{1,0:T(8,128)S(1)} %bitcast.10, f32[32,128]{1,0:T(8,128)S(1)} %copy-done.5, f32[32,128]{1,0:T(8,128)S(1)} %copy-done.4, bf16[2,2,256,256]{3,2,1,0:T(8,128)(2,1)S(1)} %copy-done.1), custom_call_target="tpu_custom_call" | custom-call | tf_op jit(solution)/shard_map/pallas_call | solution.py:477
Async XLA Ops:
  3.6 60.2 %copy-start.2 = (bf16[2,256,256]{2,1,0:T(8,128)(2,1)S(1)}, bf16[2,256,256]{2,1,0:T(8,128)(2,1)}, u32[]{:S(2)}) copy-start(bf16[2,256,256]{2,1,0:T(8,128)(2,1)} %constant.19.clone.wi_ref) | copy-start | bytes 786436
  3.6 60.2 %copy-start.3 = (bf16[2,256,256]{2,1,0:T(8,128)(2,1)S(1)}, bf16[2,256,256]{2,1,0:T(8,128)(2,1)}, u32[]{:S(2)}) copy-start(bf16[2,256,256]{2,1,0:T(8,128)(2,1)} %constant.18.clone.w_ref) | copy-start | bytes 786436
  3.6 60.2 %copy-start.4 = (f32[32,128]{1,0:T(8,128)S(1)}, f32[32,128]{1,0:T(8,128)}, u32[]{:S(2)}) copy-start(f32[32,128]{1,0:T(8,128)} %constant.17.clone.ts_ref) | copy-start | bytes 49156
  3.6 60.2 %copy-start.5 = (f32[32,128]{1,0:T(8,128)S(1)}, f32[32,128]{1,0:T(8,128)}, u32[]{:S(2)}) copy-start(f32[32,128]{1,0:T(8,128)} %constant.16.clone.tc_ref) | copy-start | bytes 49156
  67.6 42.5 %copy-start = (bf16[1,64,4096]{2,1,0:T(8,128)(2,1)S(1)}, bf16[1,64,4096]{2,1,0:T(8,128)(2,1)}, u32[]{:S(2)}) copy-start(bf16[1,64,4096]{2,1,0:T(8,128)(2,1)} %param.13) | copy-start | bytes 1572868
  67.6 42.5 %copy-start.1 = (bf16[2,2,256,256]{3,2,1,0:T(8,128)(2,1)S(1)}, bf16[2,2,256,256]{3,2,1,0:T(8,128)(2,1)}, u32[]{:S(2)}) copy-start(bf16[2,2,256,256]{3,2,1,0:T(8,128)(2,1)} %constant.20.clone.wi_ref) | copy-start | bytes 1572868

commit v5 on v4

--- a/solution.py
+++ b/solution.py
@@ -1,4 +1,3 @@
-import functools
 import math
 
 import jax
@@ -23,7 +22,6 @@
 F32 = jnp.float32
 BF16 = jnp.bfloat16
 VMEM_LIMIT = 48 * 1024 * 1024
-PRODUCT_ROWS = 512
 
 
 def split_np(table):
@@ -206,36 +204,38 @@
     for a in range(32):
         mask_ref[a : a + 1, :] = jnp.full((1, 128), hits_ref[a], F32)
 
-    def group(masked, g, carry):
-        rows = pl.ds(pl.multiple_of(g * 16 + (0 if masked else ROWS), 16), 16)
+    def group(masked, g):
+        start = g * 16 + (0 if masked else ROWS)
+        rows = slice(start, start + 16)
         values = []
         for a in range(32):
             tile = src_ref[rows, a * TILE : (a + 1) * TILE].astype(F32)
             values.append(tile * mask_ref[a : a + 1, :] if masked else tile)
         base = g * 16 + (0 if masked else 1024)
         spec = real_forward(values)
-        at = pl.ds(pl.multiple_of(base, 16), 16)
+        at = slice(base, base + 16)
         y_ref[at, :128] = spec[0][0]
         y_ref[at, 128:] = spec[16][0]
         for k in range(1, 16):
-            at = pl.ds(pl.multiple_of(base + k * ROWS, 16), 16)
+            at = slice(base + k * ROWS, base + k * ROWS + 16)
             re, im = spec[k]
             c, s = tw[k : k + 1, :], tw[32 + k : 33 + k, :]
             y_ref[at, :128] = re * c + im * s
             y_ref[at, 128:] = im * c - re * s
-        return carry
 
     copies[1].wait()
     copies[2].wait()
-    lax.fori_loop(0, 4, functools.partial(group, True), 0)
+    for g in range(4):
+        group(True, g)
     copies[3].wait()
-    lax.fori_loop(0, 4, functools.partial(group, False), 0)
     copies[4].wait()
 
     def apply(start, size, high, low):
         w_high, w_low = wt_ref[0, pl.ds(start, size), :], wt_ref[1, pl.ds(start, size), :]
         return mm(w_high, high, True) + (mm(w_high, low, True) + mm(w_low, high, True))
 
+    for g in range(4):
+        group(False, g)
     for sg in range(4):
         high, low = parts(y_ref[sg * 256 : (sg + 1) * 256, :])
         o = apply(0, 256, high, low)
@@ -290,7 +290,7 @@
         return jnp.where(left, p, middle), jnp.where(left, middle, q)
 
     def x_at(g, a, c):
-        return pl.ds(pl.multiple_of(g * 512 + a * 16 + c * 8, 8), 8)
+        return slice(g * 512 + a * 16 + c * 8, g * 512 + a * 16 + c * 8 + 8)
 
     def received(a, upper, q):
         return in_ref[pl.ds(a * 80 + upper * 40 + q, 8, stride=5), :]
@@ -318,41 +318,33 @@
         squared = uy * uy + ux * ux
         bend_ref[g * 32 : (g + 1) * 32, :] = squared / (1.0 + jnp.sqrt(1.0 - squared))
 
-    def forward(h, carry):
-        packed = jnp.logical_and(jnp.logical_and(first, h == 0), left)
+    def forward(h):
+        packed = jnp.logical_and(first, left)
         halves = []
         for upper in range(2):
             values = []
             for a in range(32):
                 re, im = received(a, upper, h), received(a, upper, 2 + h)
-                values.append((re, jnp.where(packed, zero, im)))
+                values.append((re, jnp.where(packed, zero, im) if h == 0 else im))
             halves.append(complex_sum(values, -1))
         for k in range(32):
             lower, upper = halves[0][k], halves[1][k]
             for number, column in enumerate(zip(*[exchanged(p, q) for p, q in zip(lower, upper)])):
                 store_spectrum(2 * h + number, k, *column)
-        return carry
-
-    lax.fori_loop(0, 2, forward, 0)
-
-    def gather(a, carry):
+
+
+    for a in range(32):
         both = jnp.where(left, received(a, 0, 4), swap(received(a, 1, 4)))
         x_ref[x_at(0, a, 0), :] = both
         x_ref[x_at(0, a, 1), :] = jnp.where(jnp.logical_and(first, fourth), zero, pltpu.roll(both, 4, 0))
         both = jnp.where(left, received(a, 0, 2), swap(received(a, 1, 2)))
         x_ref[x_at(1, a, 0), :] = jnp.where(first, both, zero)
         x_ref[x_at(1, a, 1), :] = zero
-        return carry
-
-    lax.fori_loop(0, 32, gather, 0, unroll=8)
-
-    def forward_extra(g, carry):
+
+    for g in range(2):
         values = [(x_ref[x_at(g, a, 0), :], x_ref[x_at(g, a, 1), :]) for a in range(32)]
         for k, (re, im) in enumerate(complex_sum(values, -1)):
             store_spectrum(4 + g, k, re, im)
-        return carry
-
-    lax.fori_loop(0, 2, forward_extra, 0)
 
     def product(start, size, table):
         slabs = [slice((r // 32) * 40, (r // 32) * 40 + 32) for r in range(start, start + size, 32)]
@@ -364,8 +356,11 @@
             zr_ref[at, :] = value[i * 32 : (i + 1) * 32, :128]
             zi_ref[at, :] = value[i * 32 : (i + 1) * 32, 128:]
 
-    for start in range(0, 1536, PRODUCT_ROWS):
-        product(start, PRODUCT_ROWS, w_ref)
+    forward(0)
+    product(1024, 512, w_ref)
+    forward(1)
+    product(0, 512, w_ref)
+    product(512, 512, w_ref)
 
     scales = []
     for p in range(PLANES):
@@ -373,13 +368,13 @@
         scales.append(DEPTH_SCALE * jnp.where(left, swap(row), row))
     gain = STEP_SIZE * 2.0 / (N * N)
 
-    def mix(j, carry):
-        extra = None
-        for index, g in ((4, 5), (0, 0), (1, 1), (2, 2), (3, 3)):
-            bend = bend_ref[pl.ds(pl.multiple_of(index * 32 + j * 8, 8), 8), :]
+    def mix(index):
+        g = 5 if index == 4 else index
+        for j in range(4):
+            bend = bend_ref[index * 32 + j * 8 : index * 32 + j * 8 + 8, :]
             waves = [cosine(scale * bend) for scale in scales]
-            rows = [pl.ds(pl.multiple_of(g * 320 + p * 40 + j * 8, 8), 8) for p in range(PLANES)]
-            at = pl.ds(pl.multiple_of(1280 + index * 40 + j * 8, 8), 8)
+            rows = [slice(g * 320 + p * 40 + j * 8, g * 320 + p * 40 + j * 8 + 8) for p in range(PLANES)]
+            at = slice(1280 + index * 40 + j * 8, 1280 + index * 40 + j * 8 + 8)
             scaled = []
             for ref in (zr_ref, zi_ref):
                 terms = [wave * ref[row, :] for wave, row in zip(waves, rows)]
@@ -387,23 +382,26 @@
                     terms = [p + q for p, q in zip(terms[0::2], terms[1::2])]
                 scaled.append((ref[at, :] - 2.0 * terms[0]) * gain)
             if index == 4:
-                extra = [jnp.where(first, value, zero) for value in scaled], waves
-                continue
+                scaled = [jnp.where(first, value, zero) for value in scaled]
             for p, row in enumerate(rows):
                 re, im = waves[p] * scaled[0], waves[p] * scaled[1]
                 if index == 0:
-                    re = re - extra[1][p] * extra[0][1]
-                    im = im + extra[1][p] * extra[0][0]
+                    other = slice(row.start + 1600, row.stop + 1600)
+                    re, im = re - zi_ref[other, :], im + zr_ref[other, :]
                 zr_ref[row, :] = re
                 zi_ref[row, :] = im
-        return carry
-
-    lax.fori_loop(0, 4, mix, 0)
-
-    for start in range(0, 1024, PRODUCT_ROWS):
-        product(start, PRODUCT_ROWS, wi_ref)
-
-    def backward(h, carry):
+
+    mix(4)
+    mix(0)
+    product(0, 256, wi_ref)
+    mix(1)
+    product(256, 256, wi_ref)
+    mix(2)
+    product(512, 256, wi_ref)
+    mix(3)
+    product(768, 256, wi_ref)
+
+    for h in range(2):
         lower, upper = [], []
         for k in range(32):
             columns = []
@@ -421,37 +419,32 @@
             for a, (re, im) in enumerate(complex_sum(values, 1)):
                 out_ref[pl.ds(a * 64 + number * 32 + h, 8, stride=4), :] = re
                 out_ref[pl.ds(a * 64 + number * 32 + 2 + h, 8, stride=4), :] = im
-        return carry
-
-    lax.fori_loop(0, 2, backward, 0)
-
-
-def update_kernel(mask_ref, vol_ref, in_ref, tc_ref, ts_ref, wi_ref, out_hbm, y_ref, new_ref, sems):
+
+
+def update_kernel(mask_ref, vol_ref, in_ref, tc_ref, ts_ref, wi_ref, out_hbm, y_ref, high_ref, low_ref, new_ref, sems):
     def apply(which, high, low):
         w_high, w_low = wi_ref[0, which], wi_ref[1, which]
         return mm(high, w_high) + (mm(low, w_high) + mm(high, w_low))
 
     for sg in range(4):
-        for h in range(2):
-            blocks = [in_ref[pl.ds(sg * 512 + c * 2 + h, 128, stride=4), :].T for c in range(2)]
-            high, low = parts(jnp.concatenate(blocks, axis=1))
-            slot = sg * 4 + h * 2
-            if slot == 0:
-                y_ref[0:64, :] = apply(1, high[:64], low[:64])
-                y_ref[64:128, :] = apply(0, high[64:], low[64:])
-            else:
-                y_ref[slot * 64 : slot * 64 + 128, :] = apply(0, high, low)
+        blocks = [[in_ref[pl.ds(sg * 512 + c * 2 + h, 128, stride=4), :].T for c in range(2)] for h in range(2)]
+        high, low = parts(jnp.concatenate([jnp.concatenate(pair, axis=1) for pair in blocks], axis=0))
+        high_ref[sg * 256 : (sg + 1) * 256, :] = high
+        low_ref[sg * 256 : (sg + 1) * 256, :] = low
+    y_ref[0:64, :] = apply(1, high_ref[0:64, :], low_ref[0:64, :])
 
     def copy_out(g):
-        rows = pl.ds(pl.multiple_of(g * 16, 16), 16)
+        rows = slice(g * 16, g * 16 + 16)
         return pltpu.make_async_copy(new_ref.at[rows], out_hbm.at[rows], sems.at[g])
 
-    def group(g, carry):
-        rows = pl.ds(pl.multiple_of(g * 16, 16), 16)
+    for g in range(4):
+        rows = slice(g * 16, g * 16 + 16)
+        spots = [slice(g * 16 + k * ROWS, g * 16 + k * ROWS + 16) for k in range(1, 16)]
+        value = apply(0, *[jnp.concatenate([ref[at, :] for at in spots], axis=0) for ref in (high_ref, low_ref)])
         spec = [(y_ref[rows, :128], None)]
         for k in range(1, 16):
-            at = pl.ds(pl.multiple_of(g * 16 + k * ROWS, 16), 16)
-            re, im = y_ref[at, :128], y_ref[at, 128:]
+            at = slice((k - 1) * 16, k * 16)
+            re, im = value[at, :128], value[at, 128:]
             c, s = tc_ref[k : k + 1, :], ts_ref[k : k + 1, :]
             spec.append((re * c - im * s, im * c + re * s))
         spec.append((y_ref[rows, 128:], None))
@@ -461,9 +454,6 @@
             updated = vol_ref[rows, cols].astype(F32) * support + step
             new_ref[rows, cols] = support * (updated - jnp.clip(updated, -THRESHOLD, THRESHOLD))
         copy_out(g).start()
-        return carry
-
-    lax.fori_loop(0, 4, group, 0)
     for g in range(4):
         copy_out(g).wait()
 
@@ -527,7 +517,7 @@
         [(ROWS, N)],
         (mask, volume, received, tc, ts, wi),
         "vvvvvvh",
-        [pltpu.VMEM((1024, 256), F32), pltpu.VMEM((ROWS, N), F32), pltpu.SemaphoreType.DMA((4,))],
+        [pltpu.VMEM((64, 256), F32), pltpu.VMEM((1024, 256), BF16), pltpu.VMEM((1024, 256), BF16), pltpu.VMEM((ROWS, N), F32), pltpu.SemaphoreType.DMA((4,))],
     )
 
 

time: 112 us -> 111 us (level)
  Pallas kernels: 8.79 us -> 7.43 us
    pallas_call x3, Pallas kernels: 8.79 us -> 7.43 us  [call(): pl.pallas_call(kernel, out_shape=[jax.ShapeDtypeStruct(shape, F32) for sh...]
where the time goes in v5:
time: 111 us
  blocking collectives  103 us (93%)
  Pallas kernels  7.43 us (7%)
    all_to_all x2, blocking collectives, exchange(): lax.all_to_all(value.reshape(shape), ('lat', 'depth'), split_axis=0, conc...  103 us
    pallas_call x3, Pallas kernels, call(): pl.pallas_call(kernel, out_shape=[jax.ShapeDtypeStruct(shape, F32) for sh...  7.43 us

profile of v5, /device:TPU:1, one launch (start us, length us, event | category | flops | bytes accessed | tf_op | source)
XLA Modules:
  0.0 110.8 jit_solution(9980317966415235929)
XLA Ops:
  0.7 2.8 %shard_map.127 = (f32[2560,128]{1,0:T(8,128)S(1)}, f32[32,128]{1,0:T(8,128)S(1)}) custom-call(f32[1]{0:T(128)S(6)} %copy.15.depth_ref, s32[16,32]{1,0:T(8,128)} %bitcast.15, bf16[64,4096]{1,0:T(8,128)(2,1)} %bitcast.12, bf16[64,4096]{1,0:T(8,128)(2,1)} %holo_hbm.1, f32[64,128]{1,0:T(8,128)} %constant.14.clone.tw_hbm, bf16[2,512,256]{2,1,0:T(8,128)(2,1)} %constant.15.clone.wt_hbm), custom_call_target="tpu_custom_call" | custom-call | tf_op jit(solution)/shard_map/pallas_call | solution.py:467
  3.4 0.0 copy-start.2
  3.4 0.0 copy-start.3
  3.5 0.0 copy-start.4
  3.5 0.0 copy-start.5
  3.5 60.1 %all_to_all.10 = f32[512,1,640]{2,1,0:T(1,128)S(1)} all-to-all(f32[512,1,640]{2,1,0:T(1,128)S(1)} %bitcast.14), channel_id=1, replica_groups=mesh['depth'=8,'lat'=64] {'lat','depth'}, dimensions={0} | all-to-all | bytes 2621440 | tf_op jit(solution)/shard_map/all_to_all | solution.py:525
  63.6 0.0 copy-done.2
  63.6 0.0 copy-done.3
  63.6 0.0 copy-done.4
  63.6 0.0 copy-done.5
  63.7 2.8 %shard_map.128 = f32[2048,128]{1,0:T(8,128)S(1)} custom-call(f32[2560,128]{1,0:T(8,128)S(1)} %bitcast.9, f32[32,128]{1,0:T(8,128)S(1)} %copy-done.5, f32[32,128]{1,0:T(8,128)S(1)} %copy-done.4, bf16[2,256,256]{2,1,0:T(8,128)(2,1)S(1)} %copy-done.3, bf16[2,256,256]{2,1,0:T(8,128)(2,1)S(1)} %copy-done.2), custom_call_target="tpu_custom_call" | custom-call | tf_op jit(solution)/shard_map/pallas_call | solution.py:467
  66.4 0.0 copy-start
  66.4 0.0 copy-start.1
  66.5 42.4 %all_to_all.11 = f32[512,4,128]{2,1,0:T(4,128)S(1)} all-to-all(f32[512,4,128]{2,1,0:T(4,128)S(1)} %bitcast.11), channel_id=1, replica_groups=mesh['depth'=8,'lat'=64] {'lat','depth'}, dimensions={0} | all-to-all | bytes 2097152 | tf_op jit(solution)/shard_map/all_to_all | solution.py:525
  108.9 0.0 copy-done
  108.9 0.0 copy-done.1
  108.9 1.9 %shard_map.129 = f32[64,4096]{1,0:T(8,128)} custom-call(f32[32,128]{1,0:T(8,128)S(1)} %get-tuple-element.7.mask_ref, bf16[64,4096]{1,0:T(8,128)(2,1)S(1)} %bitcast.13, f32[2048,128]{1,0:T(8,128)S(1)} %bitcast.10, f32[32,128]{1,0:T(8,128)S(1)} %copy-done.5, f32[32,128]{1,0:T(8,128)S(1)} %copy-done.4, bf16[2,2,256,256]{3,2,1,0:T(8,128)(2,1)S(1)} %copy-done.1), custom_call_target="tpu_custom_call" | custom-call | tf_op jit(solution)/shard_map/pallas_call | solution.py:467
Async XLA Ops:
  3.4 60.2 %copy-start.2 = (bf16[2,256,256]{2,1,0:T(8,128)(2,1)S(1)}, bf16[2,256,256]{2,1,0:T(8,128)(2,1)}, u32[]{:S(2)}) copy-start(bf16[2,256,256]{2,1,0:T(8,128)(2,1)} %constant.19.clone.wi_ref) | copy-start | bytes 786436
  3.4 60.2 %copy-start.3 = (bf16[2,256,256]{2,1,0:T(8,128)(2,1)S(1)}, bf16[2,256,256]{2,1,0:T(8,128)(2,1)}, u32[]{:S(2)}) copy-start(bf16[2,256,256]{2,1,0:T(8,128)(2,1)} %constant.18.clone.w_ref) | copy-start | bytes 786436
  3.5 60.2 %copy-start.4 = (f32[32,128]{1,0:T(8,128)S(1)}, f32[32,128]{1,0:T(8,128)}, u32[]{:S(2)}) copy-start(f32[32,128]{1,0:T(8,128)} %constant.17.clone.ts_ref) | copy-start | bytes 49156
  3.5 60.2 %copy-start.5 = (f32[32,128]{1,0:T(8,128)S(1)}, f32[32,128]{1,0:T(8,128)}, u32[]{:S(2)}) copy-start(f32[32,128]{1,0:T(8,128)} %constant.16.clone.tc_ref) | copy-start | bytes 49156
  66.4 42.5 %copy-start = (bf16[1,64,4096]{2,1,0:T(8,128)(2,1)S(1)}, bf16[1,64,4096]{2,1,0:T(8,128)(2,1)}, u32[]{:S(2)}) copy-start(bf16[1,64,4096]{2,1,0:T(8,128)(2,1)} %param.13) | copy-start | bytes 1572868
  66.4 42.5 %copy-start.1 = (bf16[2,2,256,256]{3,2,1,0:T(8,128)(2,1)S(1)}, bf16[2,2,256,256]{3,2,1,0:T(8,128)(2,1)}, u32[]{:S(2)}) copy-start(bf16[2,2,256,256]{3,2,1,0:T(8,128)(2,1)} %constant.20.clone.wi_ref) | copy-start | bytes 1572868

commit v6 on v5

--- a/solution.py
+++ b/solution.py
@@ -316,7 +316,8 @@
             kx = signed(jnp.full((32, 128), kx, jnp.int32))
         ux = kx.astype(F32) * (WAVE_RATIO / N)
         squared = uy * uy + ux * ux
-        bend_ref[g * 32 : (g + 1) * 32, :] = squared / (1.0 + jnp.sqrt(1.0 - squared))
+        bending = squared / (1.0 + jnp.sqrt(1.0 - squared))
+        bend_ref[g * 32 : (g + 1) * 32, :] = 0.5 * (squared + bending * bending)
 
     def forward(h):
         packed = jnp.logical_and(first, left)

time: 111 us -> 111 us (level)
  no operation moved by 1% of the time
where the time goes in v6:
time: 111 us
  blocking collectives  103 us (93%)
  Pallas kernels  7.44 us (7%)
    all_to_all x2, blocking collectives, exchange(): lax.all_to_all(value.reshape(shape), ('lat', 'depth'), split_axis=0, conc...  103 us
    pallas_call x3, Pallas kernels, call(): pl.pallas_call(kernel, out_shape=[jax.ShapeDtypeStruct(shape, F32) for sh...  7.44 us

profile of v6, /device:TPU:1, one launch (start us, length us, event | category | flops | bytes accessed | tf_op | source)
XLA Modules:
  0.0 110.8 jit_solution(8925234880663988653)
XLA Ops:
  0.7 2.8 %shard_map.127 = (f32[2560,128]{1,0:T(8,128)S(1)}, f32[32,128]{1,0:T(8,128)S(1)}) custom-call(f32[1]{0:T(128)S(6)} %copy.15.depth_ref, s32[16,32]{1,0:T(8,128)} %bitcast.15, bf16[64,4096]{1,0:T(8,128)(2,1)} %bitcast.12, bf16[64,4096]{1,0:T(8,128)(2,1)} %holo_hbm.1, f32[64,128]{1,0:T(8,128)} %constant.14.clone.tw_hbm, bf16[2,512,256]{2,1,0:T(8,128)(2,1)} %constant.15.clone.wt_hbm), custom_call_target="tpu_custom_call" | custom-call | tf_op jit(solution)/shard_map/pallas_call | solution.py:468
  3.4 0.0 copy-start.2
  3.4 0.0 copy-start.3
  3.5 0.0 copy-start.4
  3.5 0.0 copy-start.5
  3.5 60.1 %all_to_all.10 = f32[512,1,640]{2,1,0:T(1,128)S(1)} all-to-all(f32[512,1,640]{2,1,0:T(1,128)S(1)} %bitcast.14), channel_id=1, replica_groups=mesh['depth'=8,'lat'=64] {'lat','depth'}, dimensions={0} | all-to-all | bytes 2621440 | tf_op jit(solution)/shard_map/all_to_all | solution.py:526
  63.6 0.0 copy-done.2
  63.6 0.0 copy-done.3
  63.6 0.0 copy-done.4
  63.6 0.0 copy-done.5
  63.7 2.8 %shard_map.128 = f32[2048,128]{1,0:T(8,128)S(1)} custom-call(f32[2560,128]{1,0:T(8,128)S(1)} %bitcast.9, f32[32,128]{1,0:T(8,128)S(1)} %copy-done.5, f32[32,128]{1,0:T(8,128)S(1)} %copy-done.4, bf16[2,256,256]{2,1,0:T(8,128)(2,1)S(1)} %copy-done.3, bf16[2,256,256]{2,1,0:T(8,128)(2,1)S(1)} %copy-done.2), custom_call_target="tpu_custom_call" | custom-call | tf_op jit(solution)/shard_map/pallas_call | solution.py:468
  66.4 0.0 copy-start
  66.4 0.0 copy-start.1
  66.5 42.4 %all_to_all.11 = f32[512,4,128]{2,1,0:T(4,128)S(1)} all-to-all(f32[512,4,128]{2,1,0:T(4,128)S(1)} %bitcast.11), channel_id=1, replica_groups=mesh['depth'=8,'lat'=64] {'lat','depth'}, dimensions={0} | all-to-all | bytes 2097152 | tf_op jit(solution)/shard_map/all_to_all | solution.py:526
  108.9 0.0 copy-done
  108.9 0.0 copy-done.1
  108.9 1.9 %shard_map.129 = f32[64,4096]{1,0:T(8,128)} custom-call(f32[32,128]{1,0:T(8,128)S(1)} %get-tuple-element.7.mask_ref, bf16[64,4096]{1,0:T(8,128)(2,1)S(1)} %bitcast.13, f32[2048,128]{1,0:T(8,128)S(1)} %bitcast.10, f32[32,128]{1,0:T(8,128)S(1)} %copy-done.5, f32[32,128]{1,0:T(8,128)S(1)} %copy-done.4, bf16[2,2,256,256]{3,2,1,0:T(8,128)(2,1)S(1)} %copy-done.1), custom_call_target="tpu_custom_call" | custom-call | tf_op jit(solution)/shard_map/pallas_call | solution.py:468
Async XLA Ops:
  3.4 60.2 %copy-start.2 = (bf16[2,256,256]{2,1,0:T(8,128)(2,1)S(1)}, bf16[2,256,256]{2,1,0:T(8,128)(2,1)}, u32[]{:S(2)}) copy-start(bf16[2,256,256]{2,1,0:T(8,128)(2,1)} %constant.19.clone.wi_ref) | copy-start | bytes 786436
  3.4 60.2 %copy-start.3 = (bf16[2,256,256]{2,1,0:T(8,128)(2,1)S(1)}, bf16[2,256,256]{2,1,0:T(8,128)(2,1)}, u32[]{:S(2)}) copy-start(bf16[2,256,256]{2,1,0:T(8,128)(2,1)} %constant.18.clone.w_ref) | copy-start | bytes 786436
  3.5 60.2 %copy-start.4 = (f32[32,128]{1,0:T(8,128)S(1)}, f32[32,128]{1,0:T(8,128)}, u32[]{:S(2)}) copy-start(f32[32,128]{1,0:T(8,128)} %constant.17.clone.ts_ref) | copy-start | bytes 49156
  3.5 60.2 %copy-start.5 = (f32[32,128]{1,0:T(8,128)S(1)}, f32[32,128]{1,0:T(8,128)}, u32[]{:S(2)}) copy-start(f32[32,128]{1,0:T(8,128)} %constant.16.clone.tc_ref) | copy-start | bytes 49156
  66.4 42.5 %copy-start = (bf16[1,64,4096]{2,1,0:T(8,128)(2,1)S(1)}, bf16[1,64,4096]{2,1,0:T(8,128)(2,1)}, u32[]{:S(2)}) copy-start(bf16[1,64,4096]{2,1,0:T(8,128)(2,1)} %param.13) | copy-start | bytes 1572868
  66.4 42.5 %copy-start.1 = (bf16[2,2,256,256]{3,2,1,0:T(8,128)(2,1)S(1)}, bf16[2,2,256,256]{3,2,1,0:T(8,128)(2,1)}, u32[]{:S(2)}) copy-start(bf16[2,2,256,256]{3,2,1,0:T(8,128)(2,1)} %constant.20.clone.wi_ref) | copy-start | bytes 1572868

commit v7 on v6

--- a/solution.py
+++ b/solution.py
@@ -361,13 +361,31 @@
     product(1024, 512, w_ref)
     forward(1)
     product(0, 512, w_ref)
-    product(512, 512, w_ref)
 
     scales = []
     for p in range(PLANES):
         row = jnp.broadcast_to(in_ref[p * 5 + 4 : p * 5 + 5, :], (8, 128))
         scales.append(DEPTH_SCALE * jnp.where(left, swap(row), row))
     gain = STEP_SIZE * 2.0 / (N * N)
+
+    def backward(h):
+        lower, upper = [], []
+        for k in range(32):
+            columns = []
+            for g in (2 * h, 2 * h + 1):
+                at = pl.ds(g * 320 + k, 8, stride=40)
+                re, im = zr_ref[at, :], zi_ref[at, :]
+                if k > 0:
+                    c, s = tc_ref[k : k + 1, :], ts_ref[k : k + 1, :]
+                    re, im = re * c - im * s, im * c + re * s
+                columns.append((re, im))
+            halves = list(zip(*[exchanged(p, q) for p, q in zip(*columns)]))
+            lower.append(halves[0])
+            upper.append(halves[1])
+        for number, values in enumerate((lower, upper)):
+            for a, (re, im) in enumerate(complex_sum(values, 1)):
+                out_ref[pl.ds(a * 64 + number * 32 + h, 8, stride=4), :] = re
+                out_ref[pl.ds(a * 64 + number * 32 + 2 + h, 8, stride=4), :] = im
 
     def mix(index):
         g = 5 if index == 4 else index
@@ -393,33 +411,17 @@
                 zi_ref[row, :] = im
 
     mix(4)
+    product(512, 512, w_ref)
     mix(0)
     product(0, 256, wi_ref)
     mix(1)
     product(256, 256, wi_ref)
     mix(2)
     product(512, 256, wi_ref)
+    backward(0)
     mix(3)
     product(768, 256, wi_ref)
-
-    for h in range(2):
-        lower, upper = [], []
-        for k in range(32):
-            columns = []
-            for g in (2 * h, 2 * h + 1):
-                at = pl.ds(g * 320 + k, 8, stride=40)
-                re, im = zr_ref[at, :], zi_ref[at, :]
-                if k > 0:
-                    c, s = tc_ref[k : k + 1, :], ts_ref[k : k + 1, :]
-                    re, im = re * c - im * s, im * c + re * s
-                columns.append((re, im))
-            halves = list(zip(*[exchanged(p, q) for p, q in zip(*columns)]))
-            lower.append(halves[0])
-            upper.append(halves[1])
-        for number, values in enumerate((lower, upper)):
-            for a, (re, im) in enumerate(complex_sum(values, 1)):
-                out_ref[pl.ds(a * 64 + number * 32 + h, 8, stride=4), :] = re
-                out_ref[pl.ds(a * 64 + number * 32 + 2 + h, 8, stride=4), :] = im
+    backward(1)
 
 
 def update_kernel(mask_ref, vol_ref, in_ref, tc_ref, ts_ref, wi_ref, out_hbm, y_ref, high_ref, low_ref, new_ref, sems):

time: 111 us -> 111 us (level)
  no operation moved by 1% of the time
where the time goes in v7:
time: 111 us
  blocking collectives  103 us (93%)
  Pallas kernels  7.44 us (7%)
    all_to_all x2, blocking collectives, exchange(): lax.all_to_all(value.reshape(shape), ('lat', 'depth'), split_axis=0, conc...  103 us
    pallas_call x3, Pallas kernels, call(): pl.pallas_call(kernel, out_shape=[jax.ShapeDtypeStruct(shape, F32) for sh...  7.44 us

profile of v7, /device:TPU:1, one launch (start us, length us, event | category | flops | bytes accessed | tf_op | source)
XLA Modules:
  0.0 110.8 jit_solution(8925234880663988653)
XLA Ops:
  0.7 2.8 %shard_map.127 = (f32[2560,128]{1,0:T(8,128)S(1)}, f32[32,128]{1,0:T(8,128)S(1)}) custom-call(f32[1]{0:T(128)S(6)} %copy.15.depth_ref, s32[16,32]{1,0:T(8,128)} %bitcast.15, bf16[64,4096]{1,0:T(8,128)(2,1)} %bitcast.12, bf16[64,4096]{1,0:T(8,128)(2,1)} %holo_hbm.1, f32[64,128]{1,0:T(8,128)} %constant.14.clone.tw_hbm, bf16[2,512,256]{2,1,0:T(8,128)(2,1)} %constant.15.clone.wt_hbm), custom_call_target="tpu_custom_call" | custom-call | tf_op jit(solution)/shard_map/pallas_call | solution.py:470
  3.4 0.0 copy-start.2
  3.4 0.0 copy-start.3
  3.5 0.0 copy-start.4
  3.5 0.0 copy-start.5
  3.5 60.1 %all_to_all.10 = f32[512,1,640]{2,1,0:T(1,128)S(1)} all-to-all(f32[512,1,640]{2,1,0:T(1,128)S(1)} %bitcast.14), channel_id=1, replica_groups=mesh['depth'=8,'lat'=64] {'lat','depth'}, dimensions={0} | all-to-all | bytes 2621440 | tf_op jit(solution)/shard_map/all_to_all | solution.py:528
  63.6 0.0 copy-done.2
  63.6 0.0 copy-done.3
  63.6 0.0 copy-done.4
  63.6 0.0 copy-done.5
  63.7 2.8 %shard_map.128 = f32[2048,128]{1,0:T(8,128)S(1)} custom-call(f32[2560,128]{1,0:T(8,128)S(1)} %bitcast.9, f32[32,128]{1,0:T(8,128)S(1)} %copy-done.5, f32[32,128]{1,0:T(8,128)S(1)} %copy-done.4, bf16[2,256,256]{2,1,0:T(8,128)(2,1)S(1)} %copy-done.3, bf16[2,256,256]{2,1,0:T(8,128)(2,1)S(1)} %copy-done.2), custom_call_target="tpu_custom_call" | custom-call | tf_op jit(solution)/shard_map/pallas_call | solution.py:470
  66.4 0.0 copy-start
  66.4 0.0 copy-start.1
  66.5 42.4 %all_to_all.11 = f32[512,4,128]{2,1,0:T(4,128)S(1)} all-to-all(f32[512,4,128]{2,1,0:T(4,128)S(1)} %bitcast.11), channel_id=1, replica_groups=mesh['depth'=8,'lat'=64] {'lat','depth'}, dimensions={0} | all-to-all | bytes 2097152 | tf_op jit(solution)/shard_map/all_to_all | solution.py:528
  108.9 0.0 copy-done
  108.9 0.0 copy-done.1
  108.9 1.9 %shard_map.129 = f32[64,4096]{1,0:T(8,128)} custom-call(f32[32,128]{1,0:T(8,128)S(1)} %get-tuple-element.7.mask_ref, bf16[64,4096]{1,0:T(8,128)(2,1)S(1)} %bitcast.13, f32[2048,128]{1,0:T(8,128)S(1)} %bitcast.10, f32[32,128]{1,0:T(8,128)S(1)} %copy-done.5, f32[32,128]{1,0:T(8,128)S(1)} %copy-done.4, bf16[2,2,256,256]{3,2,1,0:T(8,128)(2,1)S(1)} %copy-done.1), custom_call_target="tpu_custom_call" | custom-call | tf_op jit(solution)/shard_map/pallas_call | solution.py:470
Async XLA Ops:
  3.4 60.2 %copy-start.2 = (bf16[2,256,256]{2,1,0:T(8,128)(2,1)S(1)}, bf16[2,256,256]{2,1,0:T(8,128)(2,1)}, u32[]{:S(2)}) copy-start(bf16[2,256,256]{2,1,0:T(8,128)(2,1)} %constant.19.clone.wi_ref) | copy-start | bytes 786436
  3.4 60.2 %copy-start.3 = (bf16[2,256,256]{2,1,0:T(8,128)(2,1)S(1)}, bf16[2,256,256]{2,1,0:T(8,128)(2,1)}, u32[]{:S(2)}) copy-start(bf16[2,256,256]{2,1,0:T(8,128)(2,1)} %constant.18.clone.w_ref) | copy-start | bytes 786436
  3.5 60.2 %copy-start.4 = (f32[32,128]{1,0:T(8,128)S(1)}, f32[32,128]{1,0:T(8,128)}, u32[]{:S(2)}) copy-start(f32[32,128]{1,0:T(8,128)} %constant.17.clone.ts_ref) | copy-start | bytes 49156
  3.5 60.2 %copy-start.5 = (f32[32,128]{1,0:T(8,128)S(1)}, f32[32,128]{1,0:T(8,128)}, u32[]{:S(2)}) copy-start(f32[32,128]{1,0:T(8,128)} %constant.16.clone.tc_ref) | copy-start | bytes 49156
  66.4 42.5 %copy-start = (bf16[1,64,4096]{2,1,0:T(8,128)(2,1)S(1)}, bf16[1,64,4096]{2,1,0:T(8,128)(2,1)}, u32[]{:S(2)}) copy-start(bf16[1,64,4096]{2,1,0:T(8,128)(2,1)} %param.13) | copy-start | bytes 1572868
  66.4 42.5 %copy-start.1 = (bf16[2,2,256,256]{3,2,1,0:T(8,128)(2,1)S(1)}, bf16[2,2,256,256]{3,2,1,0:T(8,128)(2,1)}, u32[]{:S(2)}) copy-start(bf16[2,2,256,256]{3,2,1,0:T(8,128)(2,1)} %constant.20.clone.wi_ref) | copy-start | bytes 1572868

commit v8 on v6

--- a/solution.py
+++ b/solution.py
@@ -273,7 +273,7 @@
     return value
 
 
-def columns_kernel(in_ref, tc_ref, ts_ref, w_ref, wi_ref, out_ref, x_ref, zr_ref, zi_ref, bend_ref):
+def columns_kernel(in_ref, tc_ref, ts_ref, w_ref, wi_ref, out_ref, zr_ref, zi_ref, bend_ref):
     depth_place, lat_place = places()
     place = lat_place * PLANES + depth_place
     first = place == 0
@@ -288,9 +288,6 @@
     def exchanged(p, q):
         middle = swap(jnp.where(left, q, p))
         return jnp.where(left, p, middle), jnp.where(left, middle, q)
-
-    def x_at(g, a, c):
-        return slice(g * 512 + a * 16 + c * 8, g * 512 + a * 16 + c * 8 + 8)
 
     def received(a, upper, q):
         return in_ref[pl.ds(a * 80 + upper * 40 + q, 8, stride=5), :]
@@ -334,18 +331,21 @@
                 store_spectrum(2 * h + number, k, *column)
 
 
+    values = []
     for a in range(32):
         both = jnp.where(left, received(a, 0, 4), swap(received(a, 1, 4)))
-        x_ref[x_at(0, a, 0), :] = both
-        x_ref[x_at(0, a, 1), :] = jnp.where(jnp.logical_and(first, fourth), zero, pltpu.roll(both, 4, 0))
+        values.append((both, jnp.where(jnp.logical_and(first, fourth), zero, pltpu.roll(both, 4, 0))))
+    for k, (re, im) in enumerate(complex_sum(values, -1)):
+        store_spectrum(4, k, re, im)
+    values = []
+    for a in range(32):
         both = jnp.where(left, received(a, 0, 2), swap(received(a, 1, 2)))
-        x_ref[x_at(1, a, 0), :] = jnp.where(first, both, zero)
-        x_ref[x_at(1, a, 1), :] = zero
-
-    for g in range(2):
-        values = [(x_ref[x_at(g, a, 0), :], x_ref[x_at(g, a, 1), :]) for a in range(32)]
-        for k, (re, im) in enumerate(complex_sum(values, -1)):
-            store_spectrum(4 + g, k, re, im)
+        values.append(jnp.where(first, both, zero))
+    half = real_forward(values)
+    for k in range(32):
+        re, im = half[min(k, 32 - k)]
+        im = zero if im is None else im
+        store_spectrum(5, k, re, im if k <= 16 else -im)
 
     def product(start, size, table):
         slabs = [slice((r // 32) * 40, (r // 32) * 40 + 32) for r in range(start, start + size, 32)]
@@ -502,7 +502,6 @@
         (received, tc, ts, split_np(matrix_forward()), split_np(matrix_inverse())),
         "vvvvvv",
         [
-            pltpu.VMEM((1024, 128), F32),
             pltpu.VMEM((1920, 128), F32),
             pltpu.VMEM((1920, 128), F32),
             pltpu.VMEM((160, 128), F32),

time: 111 us -> 111 us (level)
  no operation moved by 1% of the time
where the time goes in v8:
time: 111 us
  blocking collectives  103 us (93%)
  Pallas kernels  7.4 us (7%)
    all_to_all x2, blocking collectives, exchange(): lax.all_to_all(value.reshape(shape), ('lat', 'depth'), split_axis=0, conc...  103 us
    pallas_call x3, Pallas kernels, call(): pl.pallas_call(kernel, out_shape=[jax.ShapeDtypeStruct(shape, F32) for sh...  7.4 us

profile of v8, /device:TPU:1, one launch (start us, length us, event | category | flops | bytes accessed | tf_op | source)
XLA Modules:
  0.0 110.7 jit_solution(7333756777132112429)
XLA Ops:
  0.7 2.8 %shard_map.127 = (f32[2560,128]{1,0:T(8,128)S(1)}, f32[32,128]{1,0:T(8,128)S(1)}) custom-call(f32[1]{0:T(128)S(6)} %copy.15.depth_ref, s32[16,32]{1,0:T(8,128)} %bitcast.15, bf16[64,4096]{1,0:T(8,128)(2,1)} %bitcast.12, bf16[64,4096]{1,0:T(8,128)(2,1)} %holo_hbm.1, f32[64,128]{1,0:T(8,128)} %constant.14.clone.tw_hbm, bf16[2,512,256]{2,1,0:T(8,128)(2,1)} %constant.15.clone.wt_hbm), custom_call_target="tpu_custom_call" | custom-call | tf_op jit(solution)/shard_map/pallas_call | solution.py:468
  3.4 0.0 copy-start.2
  3.4 0.0 copy-start.3
  3.5 0.0 copy-start.4
  3.5 0.0 copy-start.5
  3.5 60.1 %all_to_all.10 = f32[512,1,640]{2,1,0:T(1,128)S(1)} all-to-all(f32[512,1,640]{2,1,0:T(1,128)S(1)} %bitcast.14), channel_id=1, replica_groups=mesh['depth'=8,'lat'=64] {'lat','depth'}, dimensions={0} | all-to-all | bytes 2621440 | tf_op jit(solution)/shard_map/all_to_all | solution.py:525
  63.6 0.0 copy-done.2
  63.6 0.0 copy-done.3
  63.6 0.0 copy-done.4
  63.6 0.0 copy-done.5
  63.7 2.7 %shard_map.128 = f32[2048,128]{1,0:T(8,128)S(1)} custom-call(f32[2560,128]{1,0:T(8,128)S(1)} %bitcast.9, f32[32,128]{1,0:T(8,128)S(1)} %copy-done.5, f32[32,128]{1,0:T(8,128)S(1)} %copy-done.4, bf16[2,256,256]{2,1,0:T(8,128)(2,1)S(1)} %copy-done.3, bf16[2,256,256]{2,1,0:T(8,128)(2,1)S(1)} %copy-done.2), custom_call_target="tpu_custom_call" | custom-call | tf_op jit(solution)/shard_map/pallas_call | solution.py:468
  66.4 0.0 copy-start
  66.4 0.0 copy-start.1
  66.4 42.4 %all_to_all.11 = f32[512,4,128]{2,1,0:T(4,128)S(1)} all-to-all(f32[512,4,128]{2,1,0:T(4,128)S(1)} %bitcast.11), channel_id=1, replica_groups=mesh['depth'=8,'lat'=64] {'lat','depth'}, dimensions={0} | all-to-all | bytes 2097152 | tf_op jit(solution)/shard_map/all_to_all | solution.py:525
  108.8 0.0 copy-done
  108.8 0.0 copy-done.1
  108.9 1.9 %shard_map.129 = f32[64,4096]{1,0:T(8,128)} custom-call(f32[32,128]{1,0:T(8,128)S(1)} %get-tuple-element.7.mask_ref, bf16[64,4096]{1,0:T(8,128)(2,1)S(1)} %bitcast.13, f32[2048,128]{1,0:T(8,128)S(1)} %bitcast.10, f32[32,128]{1,0:T(8,128)S(1)} %copy-done.5, f32[32,128]{1,0:T(8,128)S(1)} %copy-done.4, bf16[2,2,256,256]{3,2,1,0:T(8,128)(2,1)S(1)} %copy-done.1), custom_call_target="tpu_custom_call" | custom-call | tf_op jit(solution)/shard_map/pallas_call | solution.py:468
Async XLA Ops:
  3.4 60.2 %copy-start.2 = (bf16[2,256,256]{2,1,0:T(8,128)(2,1)S(1)}, bf16[2,256,256]{2,1,0:T(8,128)(2,1)}, u32[]{:S(2)}) copy-start(bf16[2,256,256]{2,1,0:T(8,128)(2,1)} %constant.19.clone.wi_ref) | copy-start | bytes 786436
  3.4 60.2 %copy-start.3 = (bf16[2,256,256]{2,1,0:T(8,128)(2,1)S(1)}, bf16[2,256,256]{2,1,0:T(8,128)(2,1)}, u32[]{:S(2)}) copy-start(bf16[2,256,256]{2,1,0:T(8,128)(2,1)} %constant.18.clone.w_ref) | copy-start | bytes 786436
  3.5 60.2 %copy-start.4 = (f32[32,128]{1,0:T(8,128)S(1)}, f32[32,128]{1,0:T(8,128)}, u32[]{:S(2)}) copy-start(f32[32,128]{1,0:T(8,128)} %constant.17.clone.ts_ref) | copy-start | bytes 49156
  3.5 60.2 %copy-start.5 = (f32[32,128]{1,0:T(8,128)S(1)}, f32[32,128]{1,0:T(8,128)}, u32[]{:S(2)}) copy-start(f32[32,128]{1,0:T(8,128)} %constant.16.clone.tc_ref) | copy-start | bytes 49156
  66.4 42.5 %copy-start = (bf16[1,64,4096]{2,1,0:T(8,128)(2,1)S(1)}, bf16[1,64,4096]{2,1,0:T(8,128)(2,1)}, u32[]{:S(2)}) copy-start(bf16[1,64,4096]{2,1,0:T(8,128)(2,1)} %param.13) | copy-start | bytes 1572868
  66.4 42.4 %copy-start.1 = (bf16[2,2,256,256]{3,2,1,0:T(8,128)(2,1)S(1)}, bf16[2,2,256,256]{3,2,1,0:T(8,128)(2,1)}, u32[]{:S(2)}) copy-start(bf16[2,2,256,256]{3,2,1,0:T(8,128)(2,1)} %constant.20.clone.wi_ref) | copy-start | bytes 1572868
